TPU v7x, 512 devices: a whole 4x8x8 slice. The times are simulated.
512 devices in a mesh: kx: 8 (over x, z_lo), ky: 8 (over z_hi, core), kz: 8 (over y).
Axes of the slice: x: 4, y: 8, z: 8 (z_hi: 4, z_lo: 2; z = z_hi * 2 + z_lo), core: 2. Of those that a mesh axis runs over, the one named last changes fastest.
Arguments:
- coeffs: bfloat16 [8, 8, 8, 128, 2, 4096], P('kx', 'ky', 'kz'), may hold values from -0.62890625 to 0.62890625
- slab_maps: int32 [8, 8, 8, 3, 32], P('kx', 'ky', 'kz'), may hold values from 0 to 31, each once within a row
Outputs:
- correlations: float32 [8, 8, 8, 6, 2, 128, 128], P('kx', 'ky', 'kz')
Inputs may be any that keep to these rules, and one draw needn't show every extreme that they name: Each row slab_maps[kx, ky, kz, d, :] holds every number of 0 to 31 once.
All inputs are finite; a program needn't handle non-finite values.
Results may differ from a plain program's by a relative error of at most 0.0003.
Values may be sent and summed in bfloat16 or wider, within the bound.
No kernel may reach another device: no remote copies, remote signals or barrier semaphores. Data moves between devices by JAX's collectives and lax.ppermute only.
A program may use at most 64 MiB of HBM per device.

v0:
```python
import jax
import jax.numpy as jnp
from jax import lax
from jax.sharding import PartitionSpec as P


def passed_along(block, axis, distance):
    devices = range(lax.axis_size(axis))
    route = [((i - distance) % len(devices), i) for i in devices]
    return lax.ppermute(block, axis, route)


def permute(values, order):
    bands, parts, width = values.shape
    count = order.shape[0]
    blocks = values.reshape(bands, parts, count, width // count)
    return jnp.take(blocks, order, axis=2).reshape(bands, parts, width)


def inverse(order):
    count = order.shape[0]
    places = jnp.arange(count, dtype=jnp.int32)
    hits = order[:, None] == places[None, :]
    return jnp.sum(jnp.where(hits, places[:, None], 0), axis=0)


def product(left, right):
    return lax.dot_general(
        left, right, (((1,), (1,)), ((), ())), preferred_element_type=jnp.float32
    )


def correlation(left, right):
    real = product(left[:, 0], right[:, 0]) + product(left[:, 1], right[:, 1])
    imag = product(left[:, 0], right[:, 1]) - product(left[:, 1], right[:, 0])
    return jnp.stack([real, imag])


def per_device(coeffs, slab_maps):
    own = coeffs[0, 0, 0]
    maps = slab_maps[0, 0, 0]
    ahead_one = passed_along(own, "kx", -1)
    ahead_two = passed_along(own, "ky", -1)
    ahead_three = passed_along(own, "kz", -1)
    behind_one = passed_along(permute(own, inverse(maps[0])), "kx", 1)
    behind_two = passed_along(permute(own, inverse(maps[1])), "ky", 1)
    behind_three = passed_along(permute(own, inverse(maps[2])), "kz", 1)
    forward_one = correlation(own, permute(ahead_one, maps[0]))
    forward_two = correlation(own, permute(ahead_two, maps[1]))
    forward_three = correlation(own, permute(ahead_three, maps[2]))
    back_one = correlation(own, behind_one)
    back_two = correlation(own, behind_two)
    back_three = correlation(own, behind_three)
    result = jnp.stack([forward_one, forward_two, forward_three, back_one, back_two, back_three])
    return result[None, None, None]


def solution(mesh):
    placed = (P("kx", "ky", "kz", None, None, None), P("kx", "ky", "kz", None, None))
    return jax.shard_map(
        per_device,
        mesh=mesh,
        in_specs=placed,
        out_specs=P("kx", "ky", "kz", None, None, None, None),
        check_vma=False,
    )
```

profile of v0, /device:TPU:6, one launch (start us, length us, event | category | flops | bytes accessed | tf_op | source)
XLA Modules:
  0.0 210.2 jit_solution(7951938137939107688)
XLA Ops:
  0.0 6.2 %copy.35 = bf16[1,1,1,128,2,4096]{3,5,4,2,1,0:T(8,128)(2,1)} copy(bf16[1,1,1,128,2,4096]{5,4,3,2,1,0:T(2,128)(2,1)} %param.4) | data formatting | bytes 4194304 | tf_op args[0]
  6.2 10.4 %collective-permute-start.1 = (bf16[128,2,4096]{0,2,1:T(8,128)(2,1)}, bf16[128,2,4096]{0,2,1:T(8,128)(2,1)}, u32[]{:S(2)}, u32[]{:S(2)}) collective-permute-start(bf16[128,2,4096]{0,2,1:T(8,128)(2,1)} %bitcast.1), channel_id=1, source_target_pairs={{8,0},{16,8},{24,16},{32,24},{40,32},{48,40},{56,48},{0,56},{9,1},... | collective-permute-start | bytes 6291464 | tf_op jit(solution)/shard_map/ppermute | solution.py:10
  16.6 5.4 %collective-permute-start.2 = (bf16[128,2,4096]{0,2,1:T(8,128)(2,1)}, bf16[128,2,4096]{0,2,1:T(8,128)(2,1)}, u32[]{:S(2)}, u32[]{:S(2)}) collective-permute-start(bf16[128,2,4096]{0,2,1:T(8,128)(2,1)} %bitcast.1), channel_id=1, source_target_pairs={{1,0},{2,1},{3,2},{4,3},{5,4},{6,5},{7,6},{0,7},{9,8},{10,9},{11,1... | collective-permute-start | bytes 6291464 | tf_op jit(solution)/shard_map/ppermute | solution.py:10
  21.9 3.6 %collective-permute-start = (bf16[128,2,4096]{0,2,1:T(8,128)(2,1)}, bf16[128,2,4096]{0,2,1:T(8,128)(2,1)}, u32[]{:S(2)}, u32[]{:S(2)}) collective-permute-start(bf16[128,2,4096]{0,2,1:T(8,128)(2,1)} %bitcast.1), channel_id=1, source_target_pairs={{64,0},{128,64},{192,128},{256,192},{320,256},{384,320},{448,384},... | collective-permute-start | bytes 6291464 | tf_op jit(solution)/shard_map/ppermute | solution.py:10
  25.7 3.1 %copy.51 = bf16[128,2,32,128]{3,0,2,1:T(8,128)(2,1)S(1)} copy(bf16[128,2,32,128]{0,3,2,1:T(8,128)(2,1)} %bitcast.36) | data formatting | bytes 4194304 | tf_op jit(solution)/shard_map/reshape;squeeze | solution.py:16
  28.9 2.1 %gather_fusion.3 = bf16[32,128,2,128]{3,1,2,0:T(8,128)(2,1)} fusion(bf16[128,2,32,128]{3,0,2,1:T(8,128)(2,1)S(1)} %copy.51, s32[1024]{0:T(1024)S(1)} %pad_clamp_fusion.2), kind=kCustom, calls=%fused_computation.3.clone | custom fusion | bytes 4194432 | tf_op jit(solution)/shard_map/jit(_take)/gather | solution.py:17
  31.0 3.2 %select_bitcast_fusion.2 = bf16[128,2,32,128]{3,0,1,2:T(8,128)(2,1)} fusion(bf16[32,128,2,128]{3,1,2,0:T(8,128)(2,1)} %gather_fusion.3, pred[32]{0:T(512)(128)(4,1)S(1)} %compare_and_fusion.2), kind=kLoop, calls=%fused_computation.8 | loop fusion | flops 1048576 | bytes 4194336 | tf_op jit(solution)/shard_map/jit(_take)/select_n | solution.py:17
  34.2 4.1 %copy.52 = bf16[128,2,32,128]{0,3,2,1:T(8,128)(2,1)} copy(bf16[128,2,32,128]{3,0,1,2:T(8,128)(2,1)} %select_bitcast_fusion.2) | data formatting | bytes 4194304 | tf_op jit(solution)/shard_map/jit(_take)/select_n | solution.py:17
  38.3 2.2 %collective-permute-start.3 = (bf16[128,2,4096]{0,2,1:T(8,128)(2,1)}, bf16[128,2,4096]{0,2,1:T(8,128)(2,1)}, u32[]{:S(2)}, u32[]{:S(2)}) collective-permute-start(bf16[128,2,4096]{0,2,1:T(8,128)(2,1)} %bitcast.235), channel_id=1, source_target_pairs={{448,0},{0,64},{64,128},{128,192},{192,256},{256,320},{320,384},{3... | collective-permute-start | bytes 6291464 | tf_op jit(solution)/shard_map/ppermute | solution.py:10
  40.7 2.2 %gather_fusion.4 = bf16[32,128,2,128]{3,1,2,0:T(8,128)(2,1)} fusion(bf16[128,2,32,128]{3,0,2,1:T(8,128)(2,1)S(1)} %copy.51, s32[1024]{0:T(1024)S(1)} %get-tuple-element.22), kind=kCustom, calls=%fused_computation.4.clone | custom fusion | bytes 4194432 | tf_op jit(solution)/shard_map/jit(_take)/gather | solution.py:17
  42.9 3.2 %select_bitcast_fusion.1 = bf16[128,2,32,128]{3,0,1,2:T(8,128)(2,1)} fusion(bf16[32,128,2,128]{3,1,2,0:T(8,128)(2,1)} %gather_fusion.4, pred[32]{0:T(512)(128)(4,1)S(1)} %compare_and_fusion.1), kind=kLoop, calls=%fused_computation.7 | loop fusion | flops 1048576 | bytes 4194336 | tf_op jit(solution)/shard_map/jit(_take)/select_n | solution.py:17
  46.1 4.1 %copy.56 = bf16[128,2,32,128]{0,3,2,1:T(8,128)(2,1)} copy(bf16[128,2,32,128]{3,0,1,2:T(8,128)(2,1)} %select_bitcast_fusion.1) | data formatting | bytes 4194304 | tf_op jit(solution)/shard_map/jit(_take)/select_n | solution.py:17
  52.1 2.1 %gather_fusion.5 = bf16[32,128,2,128]{3,1,2,0:T(8,128)(2,1)} fusion(bf16[128,2,32,128]{3,0,2,1:T(8,128)(2,1)S(1)} %copy.51, s32[1024]{0:T(1024)S(1)} %get-tuple-element.21), kind=kCustom, calls=%fused_computation.5.clone | custom fusion | bytes 4194432 | tf_op jit(solution)/shard_map/jit(_take)/gather | solution.py:17
  56.1 2.9 %copy.60 = bf16[128,2,32,128]{0,3,2,1:T(8,128)(2,1)} copy(bf16[128,2,32,128]{3,0,1,2:T(8,128)(2,1)S(1)} %select_bitcast_fusion) | data formatting | bytes 4194304 | tf_op jit(solution)/shard_map/jit(_take)/select_n | solution.py:17
  61.0 4.1 %copy.42 = bf16[128,2,32,128]{3,0,2,1:T(8,128)(2,1)} copy(bf16[128,2,32,128]{0,3,2,1:T(8,128)(2,1)} %bitcast.15) | data formatting | bytes 4194304 | tf_op jit(solution)/shard_map/reshape | solution.py:16
  65.1 64.4 %collective-permute-done = bf16[128,2,4096]{0,2,1:T(8,128)(2,1)} collective-permute-done((bf16[128,2,4096]{0,2,1:T(8,128)(2,1)}, bf16[128,2,4096]{0,2,1:T(8,128)(2,1)}, u32[]{:S(2)}, u32[]{:S(2)}) %collective-permute-start) | collective-permute-done | bytes 2097184 | tf_op jit(solution)/shard_map/ppermute | solution.py:10
  129.5 4.1 %copy.36 = bf16[128,2,32,128]{3,0,2,1:T(8,128)(2,1)} copy(bf16[128,2,32,128]{0,3,2,1:T(8,128)(2,1)} %bitcast.2) | data formatting | bytes 4194304 | tf_op jit(solution)/shard_map/reshape | solution.py:16
  133.6 2.5 %gather_fusion = bf16[32,128,2,128]{3,1,2,0:T(8,128)(2,1)S(1)} fusion(bf16[128,2,32,128]{3,0,2,1:T(8,128)(2,1)} %copy.36, s32[1024]{0:T(1024)S(1)} %pad_clamp_fusion.5), kind=kCustom, calls=%fused_computation.clone | custom fusion | bytes 4194432 | tf_op jit(solution)/shard_map/jit(_take)/gather | solution.py:17
  137.8 3.1 %copy.37 = bf16[128,2,32,128]{0,3,2,1:T(8,128)(2,1)S(1)} copy(bf16[128,2,32,128]{3,0,1,2:T(8,128)(2,1)} %select_bitcast_fusion.5) | data formatting | bytes 4194304 | tf_op jit(solution)/shard_map/jit(_take)/select_n | solution.py:17
  140.9 2.5 %fusion.12 = f32[128,128]{1,0:T(8,128)S(1)} fusion(bf16[128,2,4096]{0,2,1:T(8,128)(2,1)S(1)} %bitcast.238, bf16[128,2,4096]{0,2,1:T(8,128)(2,1)} %bitcast.1), kind=kOutput, calls=%fused_computation.50 | convolution fusion | flops 134217728 | bytes 2162688 | tf_op jit(solution)/shard_map/dot_general | solution.py:28
  145.1 4.1 %copy.46 = bf16[128,2,32,128]{3,0,2,1:T(8,128)(2,1)} copy(bf16[128,2,32,128]{0,3,2,1:T(8,128)(2,1)} %bitcast.26) | data formatting | bytes 4194304 | tf_op jit(solution)/shard_map/reshape | solution.py:16
  149.3 2.5 %gather_fusion.1 = bf16[32,128,2,128]{3,1,2,0:T(8,128)(2,1)S(1)} fusion(bf16[128,2,32,128]{3,0,2,1:T(8,128)(2,1)} %copy.42, s32[1024]{0:T(1024)S(1)} %pad_clamp_fusion.4), kind=kCustom, calls=%fused_computation.1.clone | custom fusion | bytes 4194432 | tf_op jit(solution)/shard_map/jit(_take)/gather | solution.py:17
  151.8 3.7 %gather_fusion.2 = bf16[32,128,2,128]{3,1,2,0:T(8,128)(2,1)} fusion(bf16[128,2,32,128]{3,0,2,1:T(8,128)(2,1)} %copy.46, s32[1024]{0:T(1024)S(1)} %pad_clamp_fusion.3), kind=kCustom, calls=%fused_computation.2.clone | custom fusion | bytes 4194432 | tf_op jit(solution)/shard_map/jit(_take)/gather | solution.py:17
  155.5 4.1 %select_bitcast_fusion.3 = (bf16[128,2,32,128]{3,0,1,2:T(8,128)(2,1)}, bf16[128,2,32,128]{3,0,1,2:T(8,128)(2,1)}) fusion(bf16[32,128,2,128]{3,1,2,0:T(8,128)(2,1)} %gather_fusion.2, pred[32]{0:T(512)(128)(4,1)S(1)} %get-tuple-element.6, bf16[32,128,2,128]{3,1,2,0:T(8,128)(2,1)S(1)} %gather_fusion.1, pred[32]{0:T(512)(128)(4,1)S(1)} %get-tuple-element.15), kind=kLoop, calls=%fused_computation.9 | loop fusion | flops 2097152 | bytes 8388672 | tf_op jit(solution)/shard_map/jit(_take)/select_n | solution.py:17
  159.6 4.2 %copy.47 = bf16[128,2,32,128]{0,3,2,1:T(8,128)(2,1)} copy(bf16[128,2,32,128]{3,0,1,2:T(8,128)(2,1)} %get-tuple-element.19) | data formatting | bytes 4194304 | tf_op jit(solution)/shard_map/jit(_take)/select_n | solution.py:17
  163.8 2.9 %copy.43 = bf16[128,2,32,128]{0,3,2,1:T(8,128)(2,1)} copy(bf16[128,2,32,128]{3,0,1,2:T(8,128)(2,1)S(1)} %copy-done) | data formatting | bytes 4194304 | tf_op jit(solution)/shard_map/jit(_take)/select_n | solution.py:17
  166.7 2.2 %fusion.11 = f32[1,128,128]{1,2,0:T(8,128)S(1)} fusion(f32[128,128]{1,0:T(8,128)S(1)} %fusion.12, bf16[128,2,4096]{0,2,1:T(8,128)(2,1)} %bitcast.240, bf16[128,2,4096]{0,2,1:T(8,128)(2,1)} %bitcast.1), kind=kOutput, calls=%fused_computation.35 | convolution fusion | flops 134234112 | bytes 2228224 | tf_op jit(solution)/shard_map/dot_general | solution.py:28
  186.7 2.0 fusion.4
  190.8 2.0 fusion.5
  194.8 2.0 fusion.2
  198.9 2.0 fusion.3
  207.0 2.0 fusion.1
  (61 shorter events, 40.4 us)
Async XLA Ops:
  0.0 25.6 %copy-start.5 = (s32[1,1,1,3,32]{4,2,3,1,0:T(1,128)S(1)}, s32[1,1,1,3,32]{4,2,3,1,0:T(1,128)}, u32[]{:S(2)}) copy-start(s32[1,1,1,3,32]{4,2,3,1,0:T(1,128)} %param.5) | copy-start | bytes 1156
  6.2 52.9 %collective-permute-start.1 = (bf16[128,2,4096]{0,2,1:T(8,128)(2,1)}, bf16[128,2,4096]{0,2,1:T(8,128)(2,1)}, u32[]{:S(2)}, u32[]{:S(2)}) collective-permute-start(bf16[128,2,4096]{0,2,1:T(8,128)(2,1)} %bitcast.1), channel_id=1, source_target_pairs={{8,0},{16,8},{24,16},{32,24},{40,32},{48,40},{56,48},{0,56},{9,1},... | collective-permute-start | bytes 6291464 | tf_op jit(solution)/shard_map/ppermute | solution.py:10
  16.6 128.6 %collective-permute-start.2 = (bf16[128,2,4096]{0,2,1:T(8,128)(2,1)}, bf16[128,2,4096]{0,2,1:T(8,128)(2,1)}, u32[]{:S(2)}, u32[]{:S(2)}) collective-permute-start(bf16[128,2,4096]{0,2,1:T(8,128)(2,1)} %bitcast.1), channel_id=1, source_target_pairs={{1,0},{2,1},{3,2},{4,3},{5,4},{6,5},{7,6},{0,7},{9,8},{10,9},{11,1... | collective-permute-start | bytes 6291464 | tf_op jit(solution)/shard_map/ppermute | solution.py:10
  21.9 107.6 %collective-permute-start = (bf16[128,2,4096]{0,2,1:T(8,128)(2,1)}, bf16[128,2,4096]{0,2,1:T(8,128)(2,1)}, u32[]{:S(2)}, u32[]{:S(2)}) collective-permute-start(bf16[128,2,4096]{0,2,1:T(8,128)(2,1)} %bitcast.1), channel_id=1, source_target_pairs={{64,0},{128,64},{192,128},{256,192},{320,256},{384,320},{448,384},... | collective-permute-start | bytes 6291464 | tf_op jit(solution)/shard_map/ppermute | solution.py:10
  38.3 146.4 %collective-permute-start.3 = (bf16[128,2,4096]{0,2,1:T(8,128)(2,1)}, bf16[128,2,4096]{0,2,1:T(8,128)(2,1)}, u32[]{:S(2)}, u32[]{:S(2)}) collective-permute-start(bf16[128,2,4096]{0,2,1:T(8,128)(2,1)} %bitcast.235), channel_id=1, source_target_pairs={{448,0},{0,64},{64,128},{128,192},{192,256},{256,320},{320,384},{3... | collective-permute-start | bytes 6291464 | tf_op jit(solution)/shard_map/ppermute | solution.py:10
  50.2 142.7 %collective-permute-start.4 = (bf16[128,2,4096]{0,2,1:T(8,128)(2,1)}, bf16[128,2,4096]{0,2,1:T(8,128)(2,1)}, u32[]{:S(2)}, u32[]{:S(2)}) collective-permute-start(bf16[128,2,4096]{0,2,1:T(8,128)(2,1)} %bitcast.236), channel_id=1, source_target_pairs={{56,0},{0,8},{8,16},{16,24},{24,32},{32,40},{40,48},{48,56},{57,1}... | collective-permute-start | bytes 6291464 | tf_op jit(solution)/shard_map/ppermute | solution.py:10
  59.1 141.9 %collective-permute-start.5 = (bf16[128,2,4096]{0,2,1:T(8,128)(2,1)}, bf16[128,2,4096]{0,2,1:T(8,128)(2,1)}, u32[]{:S(2)}, u32[]{:S(2)}) collective-permute-start(bf16[128,2,4096]{0,2,1:T(8,128)(2,1)} %bitcast.237), channel_id=1, source_target_pairs={{7,0},{0,1},{1,2},{2,3},{3,4},{4,5},{5,6},{6,7},{15,8},{8,9},{9,10... | collective-permute-start | bytes 6291464 | tf_op jit(solution)/shard_map/ppermute | solution.py:10
  140.9 4.2 %copy-start.1 = (bf16[128,2,32,128]{0,3,2,1:T(8,128)(2,1)}, bf16[128,2,32,128]{0,3,2,1:T(8,128)(2,1)S(1)}, u32[]{:S(2)}) copy-start(bf16[128,2,32,128]{0,3,2,1:T(8,128)(2,1)S(1)} %copy.37) | copy-start | bytes 6291460
  159.6 4.3 %copy-start = (bf16[128,2,32,128]{3,0,1,2:T(8,128)(2,1)S(1)}, bf16[128,2,32,128]{3,0,1,2:T(8,128)(2,1)}, u32[]{:S(2)}) copy-start(bf16[128,2,32,128]{3,0,1,2:T(8,128)(2,1)} %get-tuple-element.20) | copy-start | bytes 6291460
  166.7 2.2 %copy-start.2 = (bf16[128,2,32,128]{0,3,2,1:T(8,128)(2,1)S(1)}, bf16[128,2,32,128]{0,3,2,1:T(8,128)(2,1)}, u32[]{:S(2)}) copy-start(bf16[128,2,32,128]{0,3,2,1:T(8,128)(2,1)} %copy-done.1) | copy-start | bytes 6291460
  169.0 1.9 copy-start.4
  174.3 3.6 %copy-start.3 = (bf16[128,2,32,128]{0,3,2,1:T(8,128)(2,1)S(1)}, bf16[128,2,32,128]{0,3,2,1:T(8,128)(2,1)}, u32[]{:S(2)}) copy-start(bf16[128,2,32,128]{0,3,2,1:T(8,128)(2,1)} %copy.47) | copy-start | bytes 6291460
where the time goes:
time: 212 us; the launch traced here: 210 us
  waiting for transfers between devices  64.4 us (30%)
  local copies, waits for them, and re-layouts  59.5 us (28%)
  matrix products  46.1 us (22%)
  starting transfers between devices  25.4 us (12%)
  other arithmetic  14.3 us (7%)
    ppermute x6, waiting for transfers between devices, passed_along(): return lax.ppermute(block, axis, route)  64.4 us
    dot_general x24, matrix products, product(): lax.dot_general(left, right, (((1,), (1,)), ((), ())), preferred_element_...  46.1 us
    ppermute x6, starting transfers between devices, passed_along(): return lax.ppermute(block, axis, route)  25.4 us
    select_n x6, local copies, waits for them, and re-layouts, permute(): return jnp.take(blocks, order, axis=2).reshape(bands, parts, width)  21.4 us
    gather x6, local copies, waits for them, and re-layouts, permute(): return jnp.take(blocks, order, axis=2).reshape(bands, parts, width)  15.3 us
    select_n x8, other arithmetic, permute(): return jnp.take(blocks, order, axis=2).reshape(bands, parts, width)  13.9 us
    reshape x3, local copies, waits for them, and re-layouts, permute(): blocks = values.reshape(bands, parts, count, width // count)  12.3 us
    unnamed x13, local copies, waits for them, and re-layouts  6.28 us
  transfers between devices with their start and end apart: 6, of which 1 were waited for; matrix products, arithmetic and copies ran while one was open for 50% of the time, Pallas kernels for 0%

commit v1 on v0

v1 whole, which is shorter than its diff:
```python
import jax
import jax.numpy as jnp
from jax import lax
from jax.experimental import pallas as pl
from jax.experimental.pallas import tpu as pltpu
from jax.sharding import PartitionSpec as P

AXES = ("kx", "ky", "kz")
BANDS, PARTS, WIDTH, SLABS, LANES = 128, 2, 4096, 32, 128
ROWS = BANDS * PARTS
BLOCKS = 4
PER = SLABS // BLOCKS
TAIL = 16
BLOCK_ROWS = PER * ROWS + TAIL
F32 = jnp.float32
NT = (((1,), (1,)), ((), ()))
VMEM = pl.BlockSpec(memory_space=pltpu.VMEM)
SMEM = pl.BlockSpec(memory_space=pltpu.SMEM)


def routes(nx, ny, nz):
    def at(a, b, c):
        return ((a % nx) * ny + b % ny) * nz + c % nz

    square, cross, along, column = [], [], [], []
    for a in range(nx):
        for b in range(ny):
            for c in range(nz):
                me, high, core = at(a, b, c), a % 2, b % 2
                if high == core:
                    square.append((me, at(a, b - 1, c) if high else at(a, b + 1, c)))
                    cross.append((me, at(a - 1, b + 1, c) if high else at(a + 1, b - 1, c)))
                    along.append((me, at(a + 2, b, c) if high else at(a - 2, b, c)))
                else:
                    square.append((me, at(a - 1, b, c) if high else at(a + 1, b, c)))
                column.append((me, at(a, b, c - 1) if core else at(a, b, c + 1)))
    return square, cross, along, column


def back(route):
    return [(t, s) for s, t in route]


def send(x, route):
    return lax.ppermute(x, AXES, route)


def pack_kernel(u_ref, maps_ref, out_ref):
    for s in range(PER):
        out_ref[s * ROWS : (s + 1) * ROWS] = u_ref[:, :, s * LANES : (s + 1) * LANES].reshape(ROWS, LANES)
    out_ref[PER * ROWS :] = maps_ref[...].astype(F32).astype(jnp.bfloat16)


def packed(u, maps):
    padded = jnp.pad(maps, ((0, TAIL - maps.shape[0]), (0, LANES - SLABS)))
    return pl.pallas_call(
        pack_kernel,
        grid=(BLOCKS,),
        in_specs=[
            pl.BlockSpec((BANDS, PARTS, WIDTH // BLOCKS), lambda i: (0, 0, i)),
            pl.BlockSpec((TAIL, LANES), lambda i: (0, 0)),
        ],
        out_specs=pl.BlockSpec((BLOCK_ROWS, LANES), lambda i: (i, 0)),
        out_shape=jax.ShapeDtypeStruct((BLOCKS * BLOCK_ROWS, LANES), jnp.bfloat16),
        compiler_params=pltpu.CompilerParams(vmem_limit_bytes=16 << 20),
        cost_estimate=pl.CostEstimate(flops=0, bytes_accessed=4 << 20, transcendentals=0),
    )(u, padded)


def slab(ref, index):
    row = index * ROWS + lax.div(index, PER) * TAIL
    return ref[pl.ds(pl.multiple_of(row, 16), ROWS), :]


def edge_kernel(flags_ref, p_ref, q_ref, t_ref, h_ref, ints, order, g_ref, s_ref, sem):
    first = flags_ref[0]

    @pl.when(flags_ref[1] == 1)
    def _():
        tail = pl.ds(PER * ROWS, TAIL)
        chosen = jnp.where(first == 1, p_ref[tail, :].astype(F32), q_ref[tail, :].astype(F32))
        ints[...] = chosen.astype(jnp.int32)
        copy = pltpu.make_async_copy(ints, order, sem)
        copy.start()
        copy.wait()
        left, right = [], []
        for s in range(SLABS):
            other = order[flags_ref[2], s]
            left.append(slab(p_ref, jnp.where(first == 1, s, other)))
            right.append(slab(q_ref, jnp.where(first == 1, other, s)))
        g = lax.dot_general(
            jnp.concatenate(left, axis=1), jnp.concatenate(right, axis=1), NT, preferred_element_type=F32
        )
        for half in range(2):
            g_ref[half] = g[:, half * LANES : (half + 1) * LANES]
        for half in range(2):
            for part in range(2):
                s_ref[part, half * LANES : (half + 1) * LANES] = g_ref[half, pl.ds(part, BANDS, stride=2), :].T
        rr, ri = s_ref[0, pl.ds(0, BANDS, stride=2), :], s_ref[0, pl.ds(1, BANDS, stride=2), :]
        ir, ii = s_ref[1, pl.ds(0, BANDS, stride=2), :], s_ref[1, pl.ds(1, BANDS, stride=2), :]
        real, imag = rr + ii, ri - ir
        h_ref[0] = real
        h_ref[1] = -imag
        t_ref[0] = real.T
        t_ref[1] = imag.T


def edge(direction, first, runs, p, q):
    flags = jnp.stack([first, runs, direction]).astype(jnp.int32)
    shape = jax.ShapeDtypeStruct((PARTS, BANDS, BANDS), F32)
    return pl.pallas_call(
        edge_kernel,
        in_specs=[SMEM, VMEM, VMEM],
        out_specs=[VMEM, VMEM],
        out_shape=[shape, shape],
        scratch_shapes=[
            pltpu.VMEM((TAIL, LANES), jnp.int32),
            pltpu.SMEM((TAIL, LANES), jnp.int32),
            pltpu.VMEM((2, ROWS, LANES), F32),
            pltpu.VMEM((2, ROWS, LANES), F32),
            pltpu.SemaphoreType.DMA,
        ],
        compiler_params=pltpu.CompilerParams(vmem_limit_bytes=16 << 20),
        cost_estimate=pl.CostEstimate(
            flops=2 * ROWS * ROWS * WIDTH, bytes_accessed=4 << 20, transcendentals=0
        ),
    )(flags, p, q)


def gather_kernel(role_ref, k1, k4, r1, r2, r3, r4, out_ref, sems):
    three = [r1.at[i] for i in range(3)]
    places = {
        0: [k1, three[0], r4, r3, r2, k4],
        1: [three[0], three[1], k4, three[2], k1, r4],
        2: [three[2], k1, r4, three[0], three[1], k4],
        3: [r3, r2, k4, k1, three[0], r4],
    }
    for role, sources in places.items():

        @pl.when(role_ref[0] == role)
        def _():
            copies = [pltpu.make_async_copy(x, out_ref.at[i], sems.at[i]) for i, x in enumerate(sources)]
            for c in copies:
                c.start()
            for c in copies:
                c.wait()


def gathered(role, *parts):
    any_ = pl.BlockSpec(memory_space=pl.ANY)
    return pl.pallas_call(
        gather_kernel,
        in_specs=[SMEM] + [any_] * len(parts),
        out_specs=any_,
        out_shape=jax.ShapeDtypeStruct((6, PARTS, BANDS, BANDS), F32),
        scratch_shapes=[pltpu.SemaphoreType.DMA((6,))],
        compiler_params=pltpu.CompilerParams(vmem_limit_bytes=4 << 20),
        cost_estimate=pl.CostEstimate(flops=0, bytes_accessed=2 << 20, transcendentals=0),
    )(role[None], *parts)


def per_device(coeffs, slab_maps):
    square, cross, along, column = routes(*(lax.axis_size(a) for a in AXES))
    high = lax.axis_index("kx") % 2
    core = lax.axis_index("ky") % 2
    hub = (high == core).astype(jnp.int32)
    one = jnp.ones_like(hub)
    own = packed(coeffs[0, 0, 0], slab_maps[0, 0, 0])
    from_square = send(own, square)
    from_cross = send(own, cross)
    from_along = send(own, along)
    from_column = send(own, column)
    t1, h1 = edge(1 - hub, 1 - core, one, own, from_square)
    t2, h2 = edge(1, high, hub, from_square, from_cross)
    t3, h3 = edge(0, 1 - high, hub, from_square, from_along)
    t4, h4 = edge(2, core, one, own, from_column)
    back_square = send(jnp.stack([h1, t2, t3]), back(square))
    back_cross = send(h2, back(cross))
    back_along = send(h3, back(along))
    back_column = send(h4, back(column))
    out = gathered(2 * high + core, t1, t4, back_square, back_cross, back_along, back_column)
    return out[None, None, None]


def solution(mesh):
    placed = (P("kx", "ky", "kz", None, None, None), P("kx", "ky", "kz", None, None))
    return jax.shard_map(
        per_device,
        mesh=mesh,
        in_specs=placed,
        out_specs=P("kx", "ky", "kz", None, None, None, None),
        check_vma=False,
    )
```

time: 212 us -> 72.6 us (0.34)
  the two profiles are of different devices: /device:TPU:6 before, /device:TPU:24 now
where the time goes in v1:
time: 72.6 us; the launch traced here: 72.1 us
  starting transfers between devices  34.3 us (47%)
  waiting for transfers between devices  17.5 us (24%)
  Pallas kernels  16.8 us (23%)
  local copies, waits for them, and re-layouts  2.28 us (3%)
  other arithmetic  1.08 us (1%)
    ppermute x8, starting transfers between devices, send(): return lax.ppermute(x, AXES, route)  34.3 us
    ppermute x8, waiting for transfers between devices, send(): return lax.ppermute(x, AXES, route)  17.5 us
    pallas_call x4, Pallas kernels, edge(): pl.pallas_call(edge_kernel, in_specs=[SMEM, VMEM, VMEM], out_specs=[VMEM,...  14.4 us
    unnamed x3, local copies, waits for them, and re-layouts  2.27 us
  transfers between devices with their start and end apart: 8, of which 3 were waited for; matrix products, arithmetic and copies ran while one was open for 1% of the time, Pallas kernels for 20%

profile of v1, /device:TPU:24, one launch (start us, length us, event | category | flops | bytes accessed | tf_op | source)
XLA Modules:
  0.0 72.1 jit_solution(2010800788749901616)
XLA Ops:
  0.0 0.7 copy.5
  0.7 0.0 copy-start
  0.7 1.6 %copy-done = bf16[1,1,1,128,2,4096]{5,4,3,2,1,0:T(2,128)(2,1)S(1)} copy-done((bf16[1,1,1,128,2,4096]{5,4,3,2,1,0:T(2,128)(2,1)S(1)}, bf16[1,1,1,128,2,4096]{5,4,3,2,1,0:T(2,128)(2,1)}, u32[]{:S(2)}) %copy-start) | copy-done | bytes 2097176
  2.3 1.4 %shard_map.28.p_ref = bf16[8256,128]{1,0:T(8,128)(2,1)S(1)} custom-call(bf16[128,2,4096]{2,1,0:T(2,128)(2,1)S(1)} %bitcast.15, s32[16,128]{1,0:T(8,128)S(1)} %pad.4.maps_ref), custom_call_target="tpu_custom_call" | custom-call | bytes 4194304 | tf_op jit(solution)/shard_map/pallas_call | solution.py:56
  3.7 1.9 %collective-permute-start = (bf16[8256,128]{1,0:T(8,128)(2,1)S(1)}, bf16[8256,128]{1,0:T(8,128)(2,1)}, u32[]{:S(2)}, u32[]{:S(2)}) collective-permute-start(bf16[8256,128]{1,0:T(8,128)(2,1)S(1)} %shard_map.28.p_ref), channel_id=1, source_target_pairs={{0,8},{1,9},{2,10},{3,11},{4,12},{5,13},{6,14},{7,15},{8,72},{9,73... | collective-permute-start | bytes 6340616 | tf_op jit(solution)/shard_map/ppermute | solution.py:45
  5.7 4.7 %collective-permute-start.3 = (bf16[8256,128]{1,0:T(8,128)(2,1)S(1)}, bf16[8256,128]{1,0:T(8,128)(2,1)}, u32[]{:S(2)}, u32[]{:S(2)}) collective-permute-start(bf16[8256,128]{1,0:T(8,128)(2,1)S(1)} %shard_map.28.p_ref), channel_id=1, source_target_pairs={{0,384},{1,385},{2,386},{3,387},{4,388},{5,389},{6,390},{7,391},{1... | collective-permute-start | bytes 6340616 | tf_op jit(solution)/shard_map/ppermute | solution.py:45
  10.3 9.5 %collective-permute-start.2 = (bf16[8256,128]{1,0:T(8,128)(2,1)S(1)}, bf16[8256,128]{1,0:T(8,128)(2,1)}, u32[]{:S(2)}, u32[]{:S(2)}) collective-permute-start(bf16[8256,128]{1,0:T(8,128)(2,1)S(1)} %shard_map.28.p_ref), channel_id=1, source_target_pairs={{0,120},{1,121},{2,122},{3,123},{4,124},{5,125},{6,126},{7,127},{1... | collective-permute-start | bytes 6340616 | tf_op jit(solution)/shard_map/ppermute | solution.py:45
  19.8 4.7 %collective-permute-start.1 = (bf16[8256,128]{1,0:T(8,128)(2,1)S(1)}, bf16[8256,128]{1,0:T(8,128)(2,1)}, u32[]{:S(2)}, u32[]{:S(2)}) collective-permute-start(bf16[8256,128]{1,0:T(8,128)(2,1)S(1)} %shard_map.28.p_ref), channel_id=1, source_target_pairs={{0,1},{1,2},{2,3},{3,4},{4,5},{5,6},{6,7},{7,0},{8,15},{9,8},{10,9... | collective-permute-start | bytes 6340616 | tf_op jit(solution)/shard_map/ppermute | solution.py:45
  24.6 0.1 pad_add_fusion.3.flags_ref
  24.6 0.1 pad_add_fusion.2.flags_ref
  24.7 0.1 fusion.flags_ref
  24.8 7.5 %collective-permute-done.q_ref.p_ref = bf16[8256,128]{1,0:T(8,128)(2,1)} collective-permute-done((bf16[8256,128]{1,0:T(8,128)(2,1)S(1)}, bf16[8256,128]{1,0:T(8,128)(2,1)}, u32[]{:S(2)}, u32[]{:S(2)}) %collective-permute-start) | collective-permute-done | bytes 2113568 | tf_op jit(solution)/shard_map/ppermute | solution.py:45
  32.3 3.3 %shard_map.29 = (f32[2,128,128]{2,1,0:T(8,128)S(1)}, f32[2,128,128]{2,1,0:T(8,128)S(1)}) custom-call(s32[3]{0:T(128)S(1)} %fusion.flags_ref, bf16[8256,128]{1,0:T(8,128)(2,1)S(1)} %shard_map.28.p_ref, bf16[8256,128]{1,0:T(8,128)(2,1)} %collective-permute-done.q_ref.p_ref), custom_call_target="tpu_custom_call" | custom-call | flops 536870912 | bytes 4194304 | tf_op jit(solution)/shard_map/pallas_call | solution.py:111
  35.6 0.0 collective-permute-done.3.q_ref
  35.6 3.9 %shard_map.32 = (f32[2,128,128]{2,1,0:T(8,128)S(1)}, f32[2,128,128]{2,1,0:T(8,128)S(1)}) custom-call(s32[3]{0:T(128)S(1)} %pad_add_fusion.3.flags_ref, bf16[8256,128]{1,0:T(8,128)(2,1)} %collective-permute-done.q_ref.p_ref, bf16[8256,128]{1,0:T(8,128)(2,1)} %collective-permute-done.3.q_ref), custom_call_target="tpu_custom_call" | custom-call | flops 536870912 | bytes 4194304 | tf_op jit(solution)/shard_map/pallas_call | solution.py:111
  39.5 4.3 %collective-permute-done.2.q_ref = bf16[8256,128]{1,0:T(8,128)(2,1)} collective-permute-done((bf16[8256,128]{1,0:T(8,128)(2,1)S(1)}, bf16[8256,128]{1,0:T(8,128)(2,1)}, u32[]{:S(2)}, u32[]{:S(2)}) %collective-permute-start.2) | collective-permute-done | bytes 2113568 | tf_op jit(solution)/shard_map/ppermute | solution.py:45
  43.8 3.9 %shard_map.31 = (f32[2,128,128]{2,1,0:T(8,128)S(1)}, f32[2,128,128]{2,1,0:T(8,128)S(1)}) custom-call(s32[3]{0:T(128)S(1)} %pad_add_fusion.2.flags_ref, bf16[8256,128]{1,0:T(8,128)(2,1)} %collective-permute-done.q_ref.p_ref, bf16[8256,128]{1,0:T(8,128)(2,1)} %collective-permute-done.2.q_ref), custom_call_target="tpu_custom_call" | custom-call | flops 536870912 | bytes 4194304 | tf_op jit(solution)/shard_map/pallas_call | solution.py:111
  47.8 0.8 %pad_maximum_fusion = f32[3,2,128,128]{3,2,1,0:T(8,128)} fusion(f32[1,2,128,128]{3,2,1,0:T(8,128)S(1)} %bitcast.17, f32[1,2,128,128]{3,2,1,0:T(8,128)S(1)} %bitcast.18, f32[1,2,128,128]{3,2,1,0:T(8,128)S(1)} %bitcast.16), kind=kLoop, calls=%fused_computation | loop fusion | flops 196608 | bytes 786432 | tf_op jit(solution)/shard_map/stack | solution.py:177
  48.5 1.9 %collective-permute-start.4 = (f32[3,2,128,128]{3,2,1,0:T(8,128)}, f32[3,2,128,128]{3,2,1,0:T(8,128)S(1)}, u32[]{:S(2)}, u32[]{:S(2)}) collective-permute-start(f32[3,2,128,128]{3,2,1,0:T(8,128)} %pad_maximum_fusion), channel_id=1, source_target_pairs={{8,0},{9,1},{10,2},{11,3},{12,4},{13,5},{14,6},{15,7},{72,8},{73,9... | collective-permute-start | bytes 1179656 | tf_op jit(solution)/shard_map/ppermute | solution.py:45
  50.4 0.1 fusion.1.flags_ref
  50.5 3.4 %collective-permute-start.6 = (f32[2,128,128]{2,1,0:T(8,128)S(1)}, f32[2,128,128]{2,1,0:T(8,128)S(1)}, u32[]{:S(2)}, u32[]{:S(2)}) collective-permute-start(f32[2,128,128]{2,1,0:T(8,128)S(1)} %get-tuple-element.19), channel_id=1, source_target_pairs={{384,0},{385,1},{386,2},{387,3},{388,4},{389,5},{390,6},{391,7},{4... | collective-permute-start | bytes 393224 | tf_op jit(solution)/shard_map/ppermute | solution.py:45
  53.9 5.9 %collective-permute-start.5 = (f32[2,128,128]{2,1,0:T(8,128)S(1)}, f32[2,128,128]{2,1,0:T(8,128)S(1)}, u32[]{:S(2)}, u32[]{:S(2)}) collective-permute-start(f32[2,128,128]{2,1,0:T(8,128)S(1)} %get-tuple-element.18), channel_id=1, source_target_pairs={{120,0},{121,1},{122,2},{123,3},{124,4},{125,5},{126,6},{127,7},{7... | collective-permute-start | bytes 393224 | tf_op jit(solution)/shard_map/ppermute | solution.py:45
  59.8 0.0 collective-permute-done.1.q_ref
  59.8 3.3 %shard_map.30 = (f32[2,128,128]{2,1,0:T(8,128)S(1)}, f32[2,128,128]{2,1,0:T(8,128)S(1)}) custom-call(s32[3]{0:T(128)S(1)} %fusion.1.flags_ref, bf16[8256,128]{1,0:T(8,128)(2,1)S(1)} %shard_map.28.p_ref, bf16[8256,128]{1,0:T(8,128)(2,1)} %collective-permute-done.1.q_ref), custom_call_target="tpu_custom_call" | custom-call | flops 536870912 | bytes 4194304 | tf_op jit(solution)/shard_map/pallas_call | solution.py:111
  63.1 2.4 %collective-permute-start.7 = (f32[2,128,128]{2,1,0:T(8,128)S(1)}, f32[2,128,128]{2,1,0:T(8,128)S(1)}, u32[]{:S(2)}, u32[]{:S(2)}) collective-permute-start(f32[2,128,128]{2,1,0:T(8,128)S(1)} %get-tuple-element.20), channel_id=1, source_target_pairs={{1,0},{2,1},{3,2},{4,3},{5,4},{6,5},{7,6},{0,7},{15,8},{8,9},{9,10... | collective-permute-start | bytes 393224 | tf_op jit(solution)/shard_map/ppermute | solution.py:45
  65.5 0.0 collective-permute-done.6.r3
  65.5 0.0 collective-permute-done.5.r2
  65.5 5.7 %collective-permute-done.7.r4 = f32[2,128,128]{2,1,0:T(8,128)S(1)} collective-permute-done((f32[2,128,128]{2,1,0:T(8,128)S(1)}, f32[2,128,128]{2,1,0:T(8,128)S(1)}, u32[]{:S(2)}, u32[]{:S(2)}) %collective-permute-start.7) | collective-permute-done | bytes 131104 | tf_op jit(solution)/shard_map/ppermute | solution.py:45
  71.2 0.0 collective-permute-done.4.r1
  71.2 0.9 %shard_map.33 = f32[6,2,128,128]{3,2,1,0:T(8,128)} custom-call(s32[1]{0:T(128)} %bitcast.role_ref, f32[2,128,128]{2,1,0:T(8,128)S(1)} %get-tuple-element.13.k1, f32[2,128,128]{2,1,0:T(8,128)S(1)} %get-tuple-element.14.k4, f32[3,2,128,128]{3,2,1,0:T(8,128)S(1)} %collective-permute-done.4.r1, f32[2,128,128]{2,1,0:T(8,128)S(1)} %collective-permute-done.5.r2, ...), custom_call_target="tpu_custom_call" | custom-call | bytes 2097152 | tf_op jit(solution)/shard_map/pallas_call | solution.py:151
  (1 shorter events, 0.0 us)
Async XLA Ops:
  0.7 1.6 %copy-start = (bf16[1,1,1,128,2,4096]{5,4,3,2,1,0:T(2,128)(2,1)S(1)}, bf16[1,1,1,128,2,4096]{5,4,3,2,1,0:T(2,128)(2,1)}, u32[]{:S(2)}) copy-start(bf16[1,1,1,128,2,4096]{5,4,3,2,1,0:T(2,128)(2,1)} %param.2) | copy-start | bytes 6291460
  3.7 28.6 %collective-permute-start = (bf16[8256,128]{1,0:T(8,128)(2,1)S(1)}, bf16[8256,128]{1,0:T(8,128)(2,1)}, u32[]{:S(2)}, u32[]{:S(2)}) collective-permute-start(bf16[8256,128]{1,0:T(8,128)(2,1)S(1)} %shard_map.28.p_ref), channel_id=1, source_target_pairs={{0,8},{1,9},{2,10},{3,11},{4,12},{5,13},{6,14},{7,15},{8,72},{9,73... | collective-permute-start | bytes 6340616 | tf_op jit(solution)/shard_map/ppermute | solution.py:45
  5.7 29.9 %collective-permute-start.3 = (bf16[8256,128]{1,0:T(8,128)(2,1)S(1)}, bf16[8256,128]{1,0:T(8,128)(2,1)}, u32[]{:S(2)}, u32[]{:S(2)}) collective-permute-start(bf16[8256,128]{1,0:T(8,128)(2,1)S(1)} %shard_map.28.p_ref), channel_id=1, source_target_pairs={{0,384},{1,385},{2,386},{3,387},{4,388},{5,389},{6,390},{7,391},{1... | collective-permute-start | bytes 6340616 | tf_op jit(solution)/shard_map/ppermute | solution.py:45
  10.3 33.5 %collective-permute-start.2 = (bf16[8256,128]{1,0:T(8,128)(2,1)S(1)}, bf16[8256,128]{1,0:T(8,128)(2,1)}, u32[]{:S(2)}, u32[]{:S(2)}) collective-permute-start(bf16[8256,128]{1,0:T(8,128)(2,1)S(1)} %shard_map.28.p_ref), channel_id=1, source_target_pairs={{0,120},{1,121},{2,122},{3,123},{4,124},{5,125},{6,126},{7,127},{1... | collective-permute-start | bytes 6340616 | tf_op jit(solution)/shard_map/ppermute | solution.py:45
  19.8 40.0 %collective-permute-start.1 = (bf16[8256,128]{1,0:T(8,128)(2,1)S(1)}, bf16[8256,128]{1,0:T(8,128)(2,1)}, u32[]{:S(2)}, u32[]{:S(2)}) collective-permute-start(bf16[8256,128]{1,0:T(8,128)(2,1)S(1)} %shard_map.28.p_ref), channel_id=1, source_target_pairs={{0,1},{1,2},{2,3},{3,4},{4,5},{5,6},{6,7},{7,0},{8,15},{9,8},{10,9... | collective-permute-start | bytes 6340616 | tf_op jit(solution)/shard_map/ppermute | solution.py:45
  48.5 22.7 %collective-permute-start.4 = (f32[3,2,128,128]{3,2,1,0:T(8,128)}, f32[3,2,128,128]{3,2,1,0:T(8,128)S(1)}, u32[]{:S(2)}, u32[]{:S(2)}) collective-permute-start(f32[3,2,128,128]{3,2,1,0:T(8,128)} %pad_maximum_fusion), channel_id=1, source_target_pairs={{8,0},{9,1},{10,2},{11,3},{12,4},{13,5},{14,6},{15,7},{72,8},{73,9... | collective-permute-start | bytes 1179656 | tf_op jit(solution)/shard_map/ppermute | solution.py:45
  50.5 15.0 %collective-permute-start.6 = (f32[2,128,128]{2,1,0:T(8,128)S(1)}, f32[2,128,128]{2,1,0:T(8,128)S(1)}, u32[]{:S(2)}, u32[]{:S(2)}) collective-permute-start(f32[2,128,128]{2,1,0:T(8,128)S(1)} %get-tuple-element.19), channel_id=1, source_target_pairs={{384,0},{385,1},{386,2},{387,3},{388,4},{389,5},{390,6},{391,7},{4... | collective-permute-start | bytes 393224 | tf_op jit(solution)/shard_map/ppermute | solution.py:45
  53.9 11.6 %collective-permute-start.5 = (f32[2,128,128]{2,1,0:T(8,128)S(1)}, f32[2,128,128]{2,1,0:T(8,128)S(1)}, u32[]{:S(2)}, u32[]{:S(2)}) collective-permute-start(f32[2,128,128]{2,1,0:T(8,128)S(1)} %get-tuple-element.18), channel_id=1, source_target_pairs={{120,0},{121,1},{122,2},{123,3},{124,4},{125,5},{126,6},{127,7},{7... | collective-permute-start | bytes 393224 | tf_op jit(solution)/shard_map/ppermute | solution.py:45
  63.1 8.1 %collective-permute-start.7 = (f32[2,128,128]{2,1,0:T(8,128)S(1)}, f32[2,128,128]{2,1,0:T(8,128)S(1)}, u32[]{:S(2)}, u32[]{:S(2)}) collective-permute-start(f32[2,128,128]{2,1,0:T(8,128)S(1)} %get-tuple-element.20), channel_id=1, source_target_pairs={{1,0},{2,1},{3,2},{4,3},{5,4},{6,5},{7,6},{0,7},{15,8},{8,9},{9,10... | collective-permute-start | bytes 393224 | tf_op jit(solution)/shard_map/ppermute | solution.py:45

commit v2 on v1

v2 whole, which is shorter than its diff:
```python
import jax
import jax.numpy as jnp
from jax import lax
from jax.experimental import pallas as pl
from jax.experimental.pallas import tpu as pltpu
from jax.sharding import PartitionSpec as P

AXES = ("kx", "ky", "kz")
BANDS, PARTS, WIDTH, SLABS, LANES = 128, 2, 4096, 32, 128
ROWS = BANDS * PARTS
BLOCKS = 8
PER = SLABS // BLOCKS
TAIL = 16
F32 = jnp.float32
COST = 1024
NT = (((1,), (1,)), ((), ()))
ANY = pl.BlockSpec(memory_space=pl.ANY)
VMEM = pl.BlockSpec(memory_space=pltpu.VMEM)
HBM = pl.BlockSpec(memory_space=pltpu.HBM)
RESULT = jax.ShapeDtypeStruct((PARTS, BANDS, BANDS), F32)
QUAD = jax.ShapeDtypeStruct((4, PARTS, BANDS, BANDS), F32)
RESULTS = jax.ShapeDtypeStruct((3, PARTS, BANDS, BANDS), F32)


def routes(nx, ny, nz):
    def at(a, b, c):
        return ((a % nx) * ny + b % ny) * nz + c % nz

    square, cross, along, lift = [], [], [], []
    for a in range(nx):
        for b in range(ny):
            for c in range(nz):
                me, high, core = at(a, b, c), a % 2, b % 2
                up = c - 1 if core else c + 1
                if high == core:
                    square.append((me, at(a, b - 1, c) if high else at(a, b + 1, c)))
                    cross.append((me, at(a - 1, b + 1, c) if high else at(a + 1, b - 1, c)))
                    along.append((me, at(a + 2, b, c) if high else at(a - 2, b, c)))
                    lift.append((me, at(a, b - 1 if core else b + 1, up)))
                else:
                    square.append((me, at(a - 1, b, c) if high else at(a + 1, b, c)))
                    cross.append((me, at(a, b, up)))
    return square, cross, along, lift


def back(route):
    return [(t, s) for s, t in route]


def send(x, route):
    return lax.ppermute(x, AXES, route)


def place():
    return lax.rem(lax.axis_index("kx"), 2), lax.rem(lax.axis_index("ky"), 2)


def pack_kernel(u_ref, maps_ref, out_ref, raw, ready, maps, ints, in_sems, out_sems, sem):
    width = PER * LANES
    loads = [
        pltpu.make_async_copy(u_ref.at[:, :, pl.ds(i * width, width)], raw.at[i], in_sems.at[i])
        for i in range(BLOCKS)
    ]
    stores = [
        pltpu.make_async_copy(ready.at[i], out_ref.at[pl.ds(i * PER * ROWS, PER * ROWS), :], out_sems.at[i])
        for i in range(BLOCKS)
    ]
    table = pltpu.make_async_copy(maps_ref, maps, sem)
    table.start()
    for c in loads:
        c.start()
    ints[...] = jnp.zeros_like(ints)
    table.wait()
    for d in range(maps.shape[0]):
        ints[d : d + 1, :SLABS] = maps[d]
    ready[BLOCKS, :TAIL, :] = ints[...].astype(F32).astype(jnp.bfloat16)
    tail = pltpu.make_async_copy(ready.at[BLOCKS, pl.ds(0, TAIL), :], out_ref.at[pl.ds(SLABS * ROWS, TAIL), :], sem)
    tail.start()
    for i in range(BLOCKS):
        loads[i].wait()
        for s in range(PER):
            ready[i, s * ROWS : (s + 1) * ROWS, :] = raw[i, :, :, s * LANES : (s + 1) * LANES].reshape(ROWS, LANES)
        stores[i].start()
    tail.wait()
    for c in stores:
        c.wait()


def packed(u, maps):
    return pl.pallas_call(
        pack_kernel,
        in_specs=[ANY, ANY],
        out_specs=ANY,
        out_shape=jax.ShapeDtypeStruct((SLABS * ROWS + TAIL, LANES), jnp.bfloat16),
        scratch_shapes=[
            pltpu.VMEM((BLOCKS, BANDS, PARTS, PER * LANES), jnp.bfloat16),
            pltpu.VMEM((BLOCKS + 1, PER * ROWS, LANES), jnp.bfloat16),
            pltpu.VMEM((maps.shape[0], 1, SLABS), jnp.int32),
            pltpu.VMEM((TAIL, LANES), jnp.int32),
            pltpu.SemaphoreType.DMA((BLOCKS,)),
            pltpu.SemaphoreType.DMA((BLOCKS,)),
            pltpu.SemaphoreType.DMA,
        ],
        compiler_params=pltpu.CompilerParams(vmem_limit_bytes=61 << 20),
        cost_estimate=pl.CostEstimate(flops=0, bytes_accessed=4 << 20, transcendentals=0),
    )(u, maps[:, None, :])


def keep_kernel(own, out_ref, sem):
    copy = pltpu.make_async_copy(own, out_ref, sem)
    copy.start()
    copy.wait()


def kept(own):
    return pl.pallas_call(
        keep_kernel,
        in_specs=[ANY],
        out_specs=VMEM,
        out_shape=jax.ShapeDtypeStruct(own.shape, own.dtype),
        scratch_shapes=[pltpu.SemaphoreType.DMA],
        compiler_params=pltpu.CompilerParams(vmem_limit_bytes=16 << 20),
        cost_estimate=pl.CostEstimate(flops=0, bytes_accessed=4 << 20, transcendentals=0),
    )(own)


def slab(ref, index):
    return ref[pl.ds(pl.multiple_of(index * ROWS, ROWS), ROWS), :]


def multiply(p_ref, q_ref, first, direction, ints, order, g_ref, s_ref, sem):
    tail = pl.ds(SLABS * ROWS, TAIL)
    ints[...] = jnp.where(first, p_ref[tail, :].astype(F32), q_ref[tail, :].astype(F32)).astype(jnp.int32)
    copy = pltpu.make_async_copy(ints, order, sem)
    copy.start()
    copy.wait()
    left, right = [], []
    for s in range(SLABS):
        other = order[direction, s]
        left.append(slab(p_ref, jnp.where(first, s, other)))
        right.append(slab(q_ref, jnp.where(first, other, s)))
    g = lax.dot_general(
        jnp.concatenate(left, axis=1), jnp.concatenate(right, axis=1), NT, preferred_element_type=F32
    )
    for half in range(2):
        g_ref[half] = g[:, half * LANES : (half + 1) * LANES]
    for half in range(2):
        for part in range(2):
            s_ref[part, half * LANES : (half + 1) * LANES] = g_ref[half, pl.ds(part, BANDS, stride=2), :].T
    rr, ri = s_ref[0, pl.ds(0, BANDS, stride=2), :], s_ref[0, pl.ds(1, BANDS, stride=2), :]
    ir, ii = s_ref[1, pl.ds(0, BANDS, stride=2), :], s_ref[1, pl.ds(1, BANDS, stride=2), :]
    return rr + ii, ri - ir


def put(t_ref, h_ref, real, imag):
    h_ref[0] = real
    h_ref[1] = -imag
    t_ref[0] = real.T
    t_ref[1] = imag.T


def square_kernel(own, square, t_ref, b_ref, *scratch):
    high, core = place()
    put(t_ref, b_ref.at[0], *multiply(own, square, core == 0, jnp.where(high == core, 0, 1), *scratch))


def cross_kernel(own, square, cross, _, b_ref, h_ref, *scratch):
    high, core = place()

    @pl.when(high == core)
    def _():
        put(b_ref.at[2], h_ref, *multiply(square, cross, high == 1, 1, *scratch))

    @pl.when(high != core)
    def _():
        put(b_ref.at[2], h_ref, *multiply(own, cross, core == 1, 2, *scratch))


def along_kernel(square, along, lift, _, b_ref, h_ref, *scratch):
    high, core = place()

    @pl.when(high == core)
    def _():
        put(b_ref.at[1], h_ref.at[0], *multiply(square, along, high == 0, 0, *scratch))

    @pl.when(high != core)
    def _():
        put(b_ref.at[1], h_ref.at[0], *multiply(square, lift, core == 0, 2, *scratch))


def multiplier(kernel, outs, buffers, results=None):
    operands = list(buffers) if results is None else [*buffers, results]
    return pl.pallas_call(
        kernel,
        in_specs=[VMEM] * len(operands),
        out_specs=[VMEM] * len(outs),
        out_shape=outs,
        input_output_aliases={} if results is None else {len(buffers): 0},
        scratch_shapes=[
            pltpu.VMEM((TAIL, LANES), jnp.int32),
            pltpu.SMEM((TAIL, LANES), jnp.int32),
            pltpu.VMEM((2, ROWS, LANES), F32),
            pltpu.VMEM((2, ROWS, LANES), F32),
            pltpu.SemaphoreType.DMA,
        ],
        compiler_params=pltpu.CompilerParams(vmem_limit_bytes=16 << 20),
        cost_estimate=pl.CostEstimate(
            flops=COST, bytes_accessed=COST, transcendentals=0
        ),
    )(*operands)


def gather_kernel(t1, mine, r_square, r_cross, r_along, r_lift, out_ref, sems):
    high, core = place()
    three = [r_square.at[i] for i in range(3)]
    r_along, r_lift = r_along.at[0], r_lift.at[0]
    places = {
        0: [t1, three[0], r_lift, r_along, r_cross, three[1]],
        1: [three[0], three[2], mine.at[2], three[1], t1, r_cross],
        2: [three[1], t1, r_cross, three[0], three[2], mine.at[2]],
        3: [r_along, r_cross, three[1], t1, three[0], r_lift],
    }
    for role, sources in places.items():

        @pl.when(2 * high + core == role)
        def _():
            copies = [pltpu.make_async_copy(x, out_ref.at[i], sems.at[i]) for i, x in enumerate(sources)]
            for c in copies:
                c.start()
            for c in copies:
                c.wait()


def gathered(*parts):
    return pl.pallas_call(
        gather_kernel,
        in_specs=[ANY] * len(parts),
        out_specs=ANY,
        out_shape=jax.ShapeDtypeStruct((6, PARTS, BANDS, BANDS), F32),
        scratch_shapes=[pltpu.SemaphoreType.DMA((6,))],
        compiler_params=pltpu.CompilerParams(vmem_limit_bytes=4 << 20),
        cost_estimate=pl.CostEstimate(flops=0, bytes_accessed=COST, transcendentals=0),
    )(*parts)


def per_device(coeffs, slab_maps):
    square, cross, along, lift = routes(*(lax.axis_size(a) for a in AXES))
    own = packed(coeffs[0, 0, 0], slab_maps[0, 0, 0])
    from_square = send(own, square)
    from_cross = send(own, cross)
    from_along = send(own, along)
    from_lift = send(own, lift)
    own = kept(own)
    t1, results = multiplier(square_kernel, [RESULT, RESULTS], [own, from_square])
    results, h3 = multiplier(along_kernel, [RESULTS, QUAD], [from_square, from_along, from_lift], results)
    results, h2 = multiplier(cross_kernel, [RESULTS, RESULT], [own, from_square, from_cross], results)
    back_cross = send(h2, back(cross))
    back_square = send(results, back(square))
    back_along = send(h3, back(along))
    back_lift = send(h3, back(lift))
    out = gathered(t1, results, back_square, back_cross, back_along, back_lift)
    return out[None, None, None]


def solution(mesh):
    placed = (P("kx", "ky", "kz", None, None, None), P("kx", "ky", "kz", None, None))
    return jax.shard_map(
        per_device,
        mesh=mesh,
        in_specs=placed,
        out_specs=P("kx", "ky", "kz", None, None, None, None),
        check_vma=False,
    )
```

time: 72.6 us -> 63.3 us (0.87)
  the two profiles are of different devices: /device:TPU:24 before, /device:TPU:6 now
where the time goes in v2:
time: 63.3 us; the launch traced here: 62.7 us
  starting transfers between devices  35.4 us (56%)
  waiting for transfers between devices  16.2 us (26%)
  Pallas kernels  9.37 us (15%)
  local copies, waits for them, and re-layouts  1.6 us (3%)
    ppermute x8, starting transfers between devices, send(): return lax.ppermute(x, AXES, route)  35.4 us
    ppermute x8, waiting for transfers between devices, send(): return lax.ppermute(x, AXES, route)  16.2 us
    pallas_call x3, Pallas kernels, multiplier(): pl.pallas_call(kernel, in_specs=[VMEM] * len(operands), out_specs=[VMEM]...  5.01 us
    pallas_call x1, Pallas kernels, packed(): pl.pallas_call(pack_kernel, in_specs=[ANY, ANY], out_specs=ANY, out_shape...  3.27 us
    unnamed x2, local copies, waits for them, and re-layouts  1.6 us
  transfers between devices with their start and end apart: 8, of which 4 were waited for; matrix products, arithmetic and copies ran while one was open for 0% of the time, Pallas kernels for 8%

profile of v2, /device:TPU:6, one launch (start us, length us, event | category | flops | bytes accessed | tf_op | source)
XLA Modules:
  0.0 62.7 jit_solution(1688500063749441059)
XLA Ops:
  0.0 3.3 %shard_map.28.own = bf16[8208,128]{1,0:T(8,128)(2,1)} custom-call(bf16[128,2,4096]{2,1,0:T(2,128)(2,1)} %bitcast.3, s32[3,1,32]{2,1,0:T(1,128)} %bitcast.4), custom_call_target="tpu_custom_call" | custom-call | bytes 4194304 | tf_op jit(solution)/shard_map/pallas_call | solution.py:90
  3.3 1.9 %collective-permute-start = (bf16[8208,128]{1,0:T(8,128)(2,1)}, bf16[8208,128]{1,0:T(8,128)(2,1)S(1)}, u32[]{:S(2)}, u32[]{:S(2)}) collective-permute-start(bf16[8208,128]{1,0:T(8,128)(2,1)} %shard_map.28.own), channel_id=1, source_target_pairs={{0,8},{1,9},{2,10},{3,11},{4,12},{5,13},{6,14},{7,15},{8,72},{9,73... | collective-permute-start | bytes 6303752 | tf_op jit(solution)/shard_map/ppermute | solution.py:51
  5.2 2.7 %collective-permute-start.2 = (bf16[8208,128]{1,0:T(8,128)(2,1)}, bf16[8208,128]{1,0:T(8,128)(2,1)S(1)}, u32[]{:S(2)}, u32[]{:S(2)}) collective-permute-start(bf16[8208,128]{1,0:T(8,128)(2,1)} %shard_map.28.own), channel_id=1, source_target_pairs={{0,384},{1,385},{2,386},{3,387},{4,388},{5,389},{6,390},{7,391},{1... | collective-permute-start | bytes 6303752 | tf_op jit(solution)/shard_map/ppermute | solution.py:51
  7.9 3.2 %collective-permute-start.3 = (bf16[8208,128]{1,0:T(8,128)(2,1)}, bf16[8208,128]{1,0:T(8,128)(2,1)S(1)}, u32[]{:S(2)}, u32[]{:S(2)}) collective-permute-start(bf16[8208,128]{1,0:T(8,128)(2,1)} %shard_map.28.own), channel_id=1, source_target_pairs={{0,9},{1,10},{2,11},{3,12},{4,13},{5,14},{6,15},{7,8},{16,25},{17,... | collective-permute-start | bytes 6303752 | tf_op jit(solution)/shard_map/ppermute | solution.py:51
  11.1 11.6 %collective-permute-start.1 = (bf16[8208,128]{1,0:T(8,128)(2,1)}, bf16[8208,128]{1,0:T(8,128)(2,1)S(1)}, u32[]{:S(2)}, u32[]{:S(2)}) collective-permute-start(bf16[8208,128]{1,0:T(8,128)(2,1)} %shard_map.28.own), channel_id=1, source_target_pairs={{0,120},{1,121},{2,122},{3,123},{4,124},{5,125},{6,126},{7,127},{8... | collective-permute-start | bytes 6303752 | tf_op jit(solution)/shard_map/ppermute | solution.py:51
  22.7 0.0 copy-start
  22.7 1.6 %copy-done = bf16[8208,128]{1,0:T(8,128)(2,1)S(1)} copy-done((bf16[8208,128]{1,0:T(8,128)(2,1)S(1)}, bf16[8208,128]{1,0:T(8,128)(2,1)}, u32[]{:S(2)}) %copy-start) | copy-done | bytes 2101272
  24.3 0.2 shard_map.29.own
  24.5 7.3 %collective-permute-done.square = bf16[8208,128]{1,0:T(8,128)(2,1)S(1)} collective-permute-done((bf16[8208,128]{1,0:T(8,128)(2,1)}, bf16[8208,128]{1,0:T(8,128)(2,1)S(1)}, u32[]{:S(2)}, u32[]{:S(2)}) %collective-permute-start) | collective-permute-done | bytes 2101280 | tf_op jit(solution)/shard_map/ppermute | solution.py:51
  31.8 1.7 %shard_map.30 = (f32[2,128,128]{2,1,0:T(8,128)S(1)}, f32[3,2,128,128]{3,2,1,0:T(8,128)S(1)}) custom-call(bf16[8208,128]{1,0:T(8,128)(2,1)S(1)} %shard_map.29.own, bf16[8208,128]{1,0:T(8,128)(2,1)S(1)} %collective-permute-done.square), custom_call_target="tpu_custom_call" | custom-call | flops 1024 | bytes 1024 | tf_op jit(solution)/shard_map/pallas_call | solution.py:193
  33.5 3.7 %collective-permute-done.2.along = bf16[8208,128]{1,0:T(8,128)(2,1)S(1)} collective-permute-done((bf16[8208,128]{1,0:T(8,128)(2,1)}, bf16[8208,128]{1,0:T(8,128)(2,1)S(1)}, u32[]{:S(2)}, u32[]{:S(2)}) %collective-permute-start.2) | collective-permute-done | bytes 2101280 | tf_op jit(solution)/shard_map/ppermute | solution.py:51
  37.2 0.0 collective-permute-done.3.lift
  37.2 1.7 %shard_map.31 = (f32[3,2,128,128]{3,2,1,0:T(8,128)S(1)}, f32[4,2,128,128]{3,2,1,0:T(8,128)S(1)}) custom-call(bf16[8208,128]{1,0:T(8,128)(2,1)S(1)} %collective-permute-done.square, bf16[8208,128]{1,0:T(8,128)(2,1)S(1)} %collective-permute-done.2.along, bf16[8208,128]{1,0:T(8,128)(2,1)S(1)} %collective-permute-done.3.lift, ...), custom_call_target="tpu_custom_call", output_to_operand_aliasing={{0}: (3, {})} | custom-call | flops 1024 | bytes 1024 | tf_op jit(solution)/shard_map/pallas_call | solution.py:193
  38.9 3.9 %collective-permute-start.6 = (f32[4,2,128,128]{3,2,1,0:T(8,128)S(1)}, f32[4,2,128,128]{3,2,1,0:T(8,128)S(1)}, u32[]{:S(2)}, u32[]{:S(2)}) collective-permute-start(f32[4,2,128,128]{3,2,1,0:T(8,128)S(1)} %get-tuple-element.16), channel_id=1, source_target_pairs={{384,0},{385,1},{386,2},{387,3},{388,4},{389,5},{390,6},{391,7},{4... | collective-permute-start | bytes 1572872 | tf_op jit(solution)/shard_map/ppermute | solution.py:51
  42.8 1.3 %collective-permute-start.7 = (f32[4,2,128,128]{3,2,1,0:T(8,128)S(1)}, f32[4,2,128,128]{3,2,1,0:T(8,128)S(1)}, u32[]{:S(2)}, u32[]{:S(2)}) collective-permute-start(f32[4,2,128,128]{3,2,1,0:T(8,128)S(1)} %get-tuple-element.16), channel_id=1, source_target_pairs={{9,0},{10,1},{11,2},{12,3},{13,4},{14,5},{15,6},{8,7},{25,16},{26,... | collective-permute-start | bytes 1572872 | tf_op jit(solution)/shard_map/ppermute | solution.py:51
  44.1 2.6 %collective-permute-done.1.cross = bf16[8208,128]{1,0:T(8,128)(2,1)S(1)} collective-permute-done((bf16[8208,128]{1,0:T(8,128)(2,1)}, bf16[8208,128]{1,0:T(8,128)(2,1)S(1)}, u32[]{:S(2)}, u32[]{:S(2)}) %collective-permute-start.1) | collective-permute-done | bytes 2101280 | tf_op jit(solution)/shard_map/ppermute | solution.py:51
  46.7 1.7 %shard_map.32 = (f32[3,2,128,128]{3,2,1,0:T(8,128)S(1)}, f32[2,128,128]{2,1,0:T(8,128)S(1)}) custom-call(bf16[8208,128]{1,0:T(8,128)(2,1)S(1)} %shard_map.29.own, bf16[8208,128]{1,0:T(8,128)(2,1)S(1)} %collective-permute-done.square, bf16[8208,128]{1,0:T(8,128)(2,1)S(1)} %collective-permute-done.1.cross, ...), custom_call_target="tpu_custom_call", output_to_operand_aliasing={{0}: (3, {})} | custom-call | flops 1024 | bytes 1024 | tf_op jit(solution)/shard_map/pallas_call | solution.py:193
  48.4 1.9 %collective-permute-start.4 = (f32[3,2,128,128]{3,2,1,0:T(8,128)S(1)}, f32[3,2,128,128]{3,2,1,0:T(8,128)S(1)}, u32[]{:S(2)}, u32[]{:S(2)}) collective-permute-start(f32[3,2,128,128]{3,2,1,0:T(8,128)S(1)} %get-tuple-element.14.mine), channel_id=1, source_target_pairs={{8,0},{9,1},{10,2},{11,3},{12,4},{13,5},{14,6},{15,7},{72,8},{73,9... | collective-permute-start | bytes 1179656 | tf_op jit(solution)/shard_map/ppermute | solution.py:51
  50.3 8.8 %collective-permute-start.5 = (f32[2,128,128]{2,1,0:T(8,128)S(1)}, f32[2,128,128]{2,1,0:T(8,128)S(1)}, u32[]{:S(2)}, u32[]{:S(2)}) collective-permute-start(f32[2,128,128]{2,1,0:T(8,128)S(1)} %get-tuple-element.15), channel_id=1, source_target_pairs={{120,0},{121,1},{122,2},{123,3},{124,4},{125,5},{126,6},{127,7},{1... | collective-permute-start | bytes 393224 | tf_op jit(solution)/shard_map/ppermute | solution.py:51
  59.1 2.6 %collective-permute-done.5.r_cross = f32[2,128,128]{2,1,0:T(8,128)S(1)} collective-permute-done((f32[2,128,128]{2,1,0:T(8,128)S(1)}, f32[2,128,128]{2,1,0:T(8,128)S(1)}, u32[]{:S(2)}, u32[]{:S(2)}) %collective-permute-start.5) | collective-permute-done | bytes 131104 | tf_op jit(solution)/shard_map/ppermute | solution.py:51
  61.8 0.0 collective-permute-done.4.r_square
  61.8 0.0 collective-permute-done.6.r_along
  61.8 0.0 collective-permute-done.7.r_lift
  61.8 0.9 %shard_map.33 = f32[6,2,128,128]{3,2,1,0:T(8,128)} custom-call(f32[2,128,128]{2,1,0:T(8,128)S(1)} %get-tuple-element.11.t1, f32[3,2,128,128]{3,2,1,0:T(8,128)S(1)} %get-tuple-element.14.mine, f32[3,2,128,128]{3,2,1,0:T(8,128)S(1)} %collective-permute-done.4.r_square, f32[2,128,128]{2,1,0:T(8,128)S(1)} %collective-permute-done.5.r_cross, ...), custom_call_target="tpu_custom_call" | custom-call | bytes 1024 | tf_op jit(solution)/shard_map/pallas_call | solution.py:235
Async XLA Ops:
  3.3 28.5 %collective-permute-start = (bf16[8208,128]{1,0:T(8,128)(2,1)}, bf16[8208,128]{1,0:T(8,128)(2,1)S(1)}, u32[]{:S(2)}, u32[]{:S(2)}) collective-permute-start(bf16[8208,128]{1,0:T(8,128)(2,1)} %shard_map.28.own), channel_id=1, source_target_pairs={{0,8},{1,9},{2,10},{3,11},{4,12},{5,13},{6,14},{7,15},{8,72},{9,73... | collective-permute-start | bytes 6303752 | tf_op jit(solution)/shard_map/ppermute | solution.py:51
  5.2 32.0 %collective-permute-start.2 = (bf16[8208,128]{1,0:T(8,128)(2,1)}, bf16[8208,128]{1,0:T(8,128)(2,1)S(1)}, u32[]{:S(2)}, u32[]{:S(2)}) collective-permute-start(bf16[8208,128]{1,0:T(8,128)(2,1)} %shard_map.28.own), channel_id=1, source_target_pairs={{0,384},{1,385},{2,386},{3,387},{4,388},{5,389},{6,390},{7,391},{1... | collective-permute-start | bytes 6303752 | tf_op jit(solution)/shard_map/ppermute | solution.py:51
  7.9 29.3 %collective-permute-start.3 = (bf16[8208,128]{1,0:T(8,128)(2,1)}, bf16[8208,128]{1,0:T(8,128)(2,1)S(1)}, u32[]{:S(2)}, u32[]{:S(2)}) collective-permute-start(bf16[8208,128]{1,0:T(8,128)(2,1)} %shard_map.28.own), channel_id=1, source_target_pairs={{0,9},{1,10},{2,11},{3,12},{4,13},{5,14},{6,15},{7,8},{16,25},{17,... | collective-permute-start | bytes 6303752 | tf_op jit(solution)/shard_map/ppermute | solution.py:51
  11.1 35.5 %collective-permute-start.1 = (bf16[8208,128]{1,0:T(8,128)(2,1)}, bf16[8208,128]{1,0:T(8,128)(2,1)S(1)}, u32[]{:S(2)}, u32[]{:S(2)}) collective-permute-start(bf16[8208,128]{1,0:T(8,128)(2,1)} %shard_map.28.own), channel_id=1, source_target_pairs={{0,120},{1,121},{2,122},{3,123},{4,124},{5,125},{6,126},{7,127},{8... | collective-permute-start | bytes 6303752 | tf_op jit(solution)/shard_map/ppermute | solution.py:51
  22.7 1.6 %copy-start = (bf16[8208,128]{1,0:T(8,128)(2,1)S(1)}, bf16[8208,128]{1,0:T(8,128)(2,1)}, u32[]{:S(2)}) copy-start(bf16[8208,128]{1,0:T(8,128)(2,1)} %shard_map.28.own) | copy-start | bytes 6303748
  38.9 22.9 %collective-permute-start.6 = (f32[4,2,128,128]{3,2,1,0:T(8,128)S(1)}, f32[4,2,128,128]{3,2,1,0:T(8,128)S(1)}, u32[]{:S(2)}, u32[]{:S(2)}) collective-permute-start(f32[4,2,128,128]{3,2,1,0:T(8,128)S(1)} %get-tuple-element.16), channel_id=1, source_target_pairs={{384,0},{385,1},{386,2},{387,3},{388,4},{389,5},{390,6},{391,7},{4... | collective-permute-start | bytes 1572872 | tf_op jit(solution)/shard_map/ppermute | solution.py:51
  42.8 18.9 %collective-permute-start.7 = (f32[4,2,128,128]{3,2,1,0:T(8,128)S(1)}, f32[4,2,128,128]{3,2,1,0:T(8,128)S(1)}, u32[]{:S(2)}, u32[]{:S(2)}) collective-permute-start(f32[4,2,128,128]{3,2,1,0:T(8,128)S(1)} %get-tuple-element.16), channel_id=1, source_target_pairs={{9,0},{10,1},{11,2},{12,3},{13,4},{14,5},{15,6},{8,7},{25,16},{26,... | collective-permute-start | bytes 1572872 | tf_op jit(solution)/shard_map/ppermute | solution.py:51
  48.4 13.4 %collective-permute-start.4 = (f32[3,2,128,128]{3,2,1,0:T(8,128)S(1)}, f32[3,2,128,128]{3,2,1,0:T(8,128)S(1)}, u32[]{:S(2)}, u32[]{:S(2)}) collective-permute-start(f32[3,2,128,128]{3,2,1,0:T(8,128)S(1)} %get-tuple-element.14.mine), channel_id=1, source_target_pairs={{8,0},{9,1},{10,2},{11,3},{12,4},{13,5},{14,6},{15,7},{72,8},{73,9... | collective-permute-start | bytes 1179656 | tf_op jit(solution)/shard_map/ppermute | solution.py:51
  50.3 11.5 %collective-permute-start.5 = (f32[2,128,128]{2,1,0:T(8,128)S(1)}, f32[2,128,128]{2,1,0:T(8,128)S(1)}, u32[]{:S(2)}, u32[]{:S(2)}) collective-permute-start(f32[2,128,128]{2,1,0:T(8,128)S(1)} %get-tuple-element.15), channel_id=1, source_target_pairs={{120,0},{121,1},{122,2},{123,3},{124,4},{125,5},{126,6},{127,7},{1... | collective-permute-start | bytes 393224 | tf_op jit(solution)/shard_map/ppermute | solution.py:51

commit v3 on v2

--- a/solution.py
+++ b/solution.py
@@ -8,7 +8,7 @@
 AXES = ("kx", "ky", "kz")
 BANDS, PARTS, WIDTH, SLABS, LANES = 128, 2, 4096, 32, 128
 ROWS = BANDS * PARTS
-BLOCKS = 8
+BLOCKS = 4
 PER = SLABS // BLOCKS
 TAIL = 16
 F32 = jnp.float32
@@ -130,13 +130,15 @@
 
 def multiply(p_ref, q_ref, first, direction, ints, order, g_ref, s_ref, sem):
     tail = pl.ds(SLABS * ROWS, TAIL)
-    ints[...] = jnp.where(first, p_ref[tail, :].astype(F32), q_ref[tail, :].astype(F32)).astype(jnp.int32)
+    chosen = jnp.where(first, p_ref[tail, :].astype(F32), q_ref[tail, :].astype(F32))
+    rows = lax.broadcasted_iota(jnp.int32, chosen.shape, 0)
+    ints[...] = jnp.sum(jnp.where(rows == direction, chosen, 0.0), axis=0, keepdims=True).astype(jnp.int32)
     copy = pltpu.make_async_copy(ints, order, sem)
     copy.start()
     copy.wait()
     left, right = [], []
     for s in range(SLABS):
-        other = order[direction, s]
+        other = order[0, s]
         left.append(slab(p_ref, jnp.where(first, s, other)))
         right.append(slab(q_ref, jnp.where(first, other, s)))
     g = lax.dot_general(
@@ -197,8 +199,8 @@
         out_shape=outs,
         input_output_aliases={} if results is None else {len(buffers): 0},
         scratch_shapes=[
-            pltpu.VMEM((TAIL, LANES), jnp.int32),
-            pltpu.SMEM((TAIL, LANES), jnp.int32),
+            pltpu.VMEM((1, LANES), jnp.int32),
+            pltpu.SMEM((1, LANES), jnp.int32),
             pltpu.VMEM((2, ROWS, LANES), F32),
             pltpu.VMEM((2, ROWS, LANES), F32),
             pltpu.SemaphoreType.DMA,
@@ -210,7 +212,7 @@
     )(*operands)
 
 
-def gather_kernel(t1, mine, r_square, r_cross, r_along, r_lift, out_ref, sems):
+def gather_kernel(t1, mine, r_square, r_cross, r_lift, r_along, out_ref, sems):
     high, core = place()
     three = [r_square.at[i] for i in range(3)]
     r_along, r_lift = r_along.at[0], r_lift.at[0]
@@ -258,7 +260,7 @@
     back_square = send(results, back(square))
     back_along = send(h3, back(along))
     back_lift = send(h3, back(lift))
-    out = gathered(t1, results, back_square, back_cross, back_along, back_lift)
+    out = gathered(t1, results, back_square, back_cross, back_lift, back_along)
     return out[None, None, None]
 
 

time: 63.3 us -> 60.6 us (0.957)
  starting transfers between devices: 35.4 us -> 33.1 us
    ppermute x8, starting transfers between devices: 35.4 us -> 33.1 us  [send(): return lax.ppermute(x, AXES, route)]
where the time goes in v3:
time: 60.6 us; the launch traced here: 60.2 us
  starting transfers between devices  33.1 us (55%)
  waiting for transfers between devices  16.5 us (27%)
  Pallas kernels  8.9 us (15%)
  local copies, waits for them, and re-layouts  1.6 us (3%)
    ppermute x8, starting transfers between devices, send(): return lax.ppermute(x, AXES, route)  33.1 us
    ppermute x8, waiting for transfers between devices, send(): return lax.ppermute(x, AXES, route)  16.5 us
    pallas_call x3, Pallas kernels, multiplier(): pl.pallas_call(kernel, in_specs=[VMEM] * len(operands), out_specs=[VMEM]...  4.66 us
    pallas_call x1, Pallas kernels, packed(): pl.pallas_call(pack_kernel, in_specs=[ANY, ANY], out_specs=ANY, out_shape...  3.15 us
    unnamed x2, local copies, waits for them, and re-layouts  1.6 us
  transfers between devices with their start and end apart: 8, of which 4 were waited for; matrix products, arithmetic and copies ran while one was open for 0% of the time, Pallas kernels for 8%

profile of v3, /device:TPU:6, one launch (start us, length us, event | category | flops | bytes accessed | tf_op | source)
XLA Modules:
  0.0 60.2 jit_solution(2472344145327526261)
XLA Ops:
  0.0 3.2 %shard_map.28.own = bf16[8208,128]{1,0:T(8,128)(2,1)} custom-call(bf16[128,2,4096]{2,1,0:T(2,128)(2,1)} %bitcast.3, s32[3,1,32]{2,1,0:T(1,128)} %bitcast.4), custom_call_target="tpu_custom_call" | custom-call | bytes 4194304 | tf_op jit(solution)/shard_map/pallas_call | solution.py:90
  3.2 1.9 %collective-permute-start = (bf16[8208,128]{1,0:T(8,128)(2,1)}, bf16[8208,128]{1,0:T(8,128)(2,1)S(1)}, u32[]{:S(2)}, u32[]{:S(2)}) collective-permute-start(bf16[8208,128]{1,0:T(8,128)(2,1)} %shard_map.28.own), channel_id=1, source_target_pairs={{0,8},{1,9},{2,10},{3,11},{4,12},{5,13},{6,14},{7,15},{8,72},{9,73... | collective-permute-start | bytes 6303752 | tf_op jit(solution)/shard_map/ppermute | solution.py:51
  5.1 2.7 %collective-permute-start.2 = (bf16[8208,128]{1,0:T(8,128)(2,1)}, bf16[8208,128]{1,0:T(8,128)(2,1)S(1)}, u32[]{:S(2)}, u32[]{:S(2)}) collective-permute-start(bf16[8208,128]{1,0:T(8,128)(2,1)} %shard_map.28.own), channel_id=1, source_target_pairs={{0,384},{1,385},{2,386},{3,387},{4,388},{5,389},{6,390},{7,391},{1... | collective-permute-start | bytes 6303752 | tf_op jit(solution)/shard_map/ppermute | solution.py:51
  7.8 3.2 %collective-permute-start.3 = (bf16[8208,128]{1,0:T(8,128)(2,1)}, bf16[8208,128]{1,0:T(8,128)(2,1)S(1)}, u32[]{:S(2)}, u32[]{:S(2)}) collective-permute-start(bf16[8208,128]{1,0:T(8,128)(2,1)} %shard_map.28.own), channel_id=1, source_target_pairs={{0,9},{1,10},{2,11},{3,12},{4,13},{5,14},{6,15},{7,8},{16,25},{17,... | collective-permute-start | bytes 6303752 | tf_op jit(solution)/shard_map/ppermute | solution.py:51
  11.0 11.6 %collective-permute-start.1 = (bf16[8208,128]{1,0:T(8,128)(2,1)}, bf16[8208,128]{1,0:T(8,128)(2,1)S(1)}, u32[]{:S(2)}, u32[]{:S(2)}) collective-permute-start(bf16[8208,128]{1,0:T(8,128)(2,1)} %shard_map.28.own), channel_id=1, source_target_pairs={{0,120},{1,121},{2,122},{3,123},{4,124},{5,125},{6,126},{7,127},{8... | collective-permute-start | bytes 6303752 | tf_op jit(solution)/shard_map/ppermute | solution.py:51
  22.6 0.0 copy-start
  22.6 1.6 %copy-done = bf16[8208,128]{1,0:T(8,128)(2,1)S(1)} copy-done((bf16[8208,128]{1,0:T(8,128)(2,1)S(1)}, bf16[8208,128]{1,0:T(8,128)(2,1)}, u32[]{:S(2)}) %copy-start) | copy-done | bytes 2101272
  24.2 0.2 shard_map.29.own
  24.4 7.3 %collective-permute-done.square = bf16[8208,128]{1,0:T(8,128)(2,1)S(1)} collective-permute-done((bf16[8208,128]{1,0:T(8,128)(2,1)}, bf16[8208,128]{1,0:T(8,128)(2,1)S(1)}, u32[]{:S(2)}, u32[]{:S(2)}) %collective-permute-start) | collective-permute-done | bytes 2101280 | tf_op jit(solution)/shard_map/ppermute | solution.py:51
  31.7 1.6 %shard_map.30 = (f32[2,128,128]{2,1,0:T(8,128)S(1)}, f32[3,2,128,128]{3,2,1,0:T(8,128)S(1)}) custom-call(bf16[8208,128]{1,0:T(8,128)(2,1)S(1)} %shard_map.29.own, bf16[8208,128]{1,0:T(8,128)(2,1)S(1)} %collective-permute-done.square), custom_call_target="tpu_custom_call" | custom-call | flops 1024 | bytes 1024 | tf_op jit(solution)/shard_map/pallas_call | solution.py:195
  33.3 3.8 %collective-permute-done.2.along = bf16[8208,128]{1,0:T(8,128)(2,1)S(1)} collective-permute-done((bf16[8208,128]{1,0:T(8,128)(2,1)}, bf16[8208,128]{1,0:T(8,128)(2,1)S(1)}, u32[]{:S(2)}, u32[]{:S(2)}) %collective-permute-start.2) | collective-permute-done | bytes 2101280 | tf_op jit(solution)/shard_map/ppermute | solution.py:51
  37.1 0.0 collective-permute-done.3.lift
  37.1 1.6 %shard_map.31 = (f32[3,2,128,128]{3,2,1,0:T(8,128)S(1)}, f32[4,2,128,128]{3,2,1,0:T(8,128)S(1)}) custom-call(bf16[8208,128]{1,0:T(8,128)(2,1)S(1)} %collective-permute-done.square, bf16[8208,128]{1,0:T(8,128)(2,1)S(1)} %collective-permute-done.2.along, bf16[8208,128]{1,0:T(8,128)(2,1)S(1)} %collective-permute-done.3.lift, ...), custom_call_target="tpu_custom_call", output_to_operand_aliasing={{0}: (3, {})} | custom-call | flops 1024 | bytes 1024 | tf_op jit(solution)/shard_map/pallas_call | solution.py:195
  38.7 1.3 %collective-permute-start.6 = (f32[4,2,128,128]{3,2,1,0:T(8,128)S(1)}, f32[4,2,128,128]{3,2,1,0:T(8,128)S(1)}, u32[]{:S(2)}, u32[]{:S(2)}) collective-permute-start(f32[4,2,128,128]{3,2,1,0:T(8,128)S(1)} %get-tuple-element.16), channel_id=1, source_target_pairs={{9,0},{10,1},{11,2},{12,3},{13,4},{14,5},{15,6},{8,7},{25,16},{26,... | collective-permute-start | bytes 1572872 | tf_op jit(solution)/shard_map/ppermute | solution.py:51
  40.0 3.9 %collective-permute-start.7 = (f32[4,2,128,128]{3,2,1,0:T(8,128)S(1)}, f32[4,2,128,128]{3,2,1,0:T(8,128)S(1)}, u32[]{:S(2)}, u32[]{:S(2)}) collective-permute-start(f32[4,2,128,128]{3,2,1,0:T(8,128)S(1)} %get-tuple-element.16), channel_id=1, source_target_pairs={{384,0},{385,1},{386,2},{387,3},{388,4},{389,5},{390,6},{391,7},{4... | collective-permute-start | bytes 1572872 | tf_op jit(solution)/shard_map/ppermute | solution.py:51
  43.9 2.7 %collective-permute-done.1.cross = bf16[8208,128]{1,0:T(8,128)(2,1)S(1)} collective-permute-done((bf16[8208,128]{1,0:T(8,128)(2,1)}, bf16[8208,128]{1,0:T(8,128)(2,1)S(1)}, u32[]{:S(2)}, u32[]{:S(2)}) %collective-permute-start.1) | collective-permute-done | bytes 2101280 | tf_op jit(solution)/shard_map/ppermute | solution.py:51
  46.6 1.5 %shard_map.32 = (f32[3,2,128,128]{3,2,1,0:T(8,128)S(1)}, f32[2,128,128]{2,1,0:T(8,128)S(1)}) custom-call(bf16[8208,128]{1,0:T(8,128)(2,1)S(1)} %shard_map.29.own, bf16[8208,128]{1,0:T(8,128)(2,1)S(1)} %collective-permute-done.square, bf16[8208,128]{1,0:T(8,128)(2,1)S(1)} %collective-permute-done.1.cross, ...), custom_call_target="tpu_custom_call", output_to_operand_aliasing={{0}: (3, {})} | custom-call | flops 1024 | bytes 1024 | tf_op jit(solution)/shard_map/pallas_call | solution.py:195
  48.1 1.9 %collective-permute-start.4 = (f32[3,2,128,128]{3,2,1,0:T(8,128)S(1)}, f32[3,2,128,128]{3,2,1,0:T(8,128)S(1)}, u32[]{:S(2)}, u32[]{:S(2)}) collective-permute-start(f32[3,2,128,128]{3,2,1,0:T(8,128)S(1)} %get-tuple-element.14.mine), channel_id=1, source_target_pairs={{8,0},{9,1},{10,2},{11,3},{12,4},{13,5},{14,6},{15,7},{72,8},{73,9... | collective-permute-start | bytes 1179656 | tf_op jit(solution)/shard_map/ppermute | solution.py:51
  50.1 6.6 %collective-permute-start.5 = (f32[2,128,128]{2,1,0:T(8,128)S(1)}, f32[2,128,128]{2,1,0:T(8,128)S(1)}, u32[]{:S(2)}, u32[]{:S(2)}) collective-permute-start(f32[2,128,128]{2,1,0:T(8,128)S(1)} %get-tuple-element.15), channel_id=1, source_target_pairs={{120,0},{121,1},{122,2},{123,3},{124,4},{125,5},{126,6},{127,7},{1... | collective-permute-start | bytes 393224 | tf_op jit(solution)/shard_map/ppermute | solution.py:51
  56.6 2.6 %collective-permute-done.5.r_cross = f32[2,128,128]{2,1,0:T(8,128)S(1)} collective-permute-done((f32[2,128,128]{2,1,0:T(8,128)S(1)}, f32[2,128,128]{2,1,0:T(8,128)S(1)}, u32[]{:S(2)}, u32[]{:S(2)}) %collective-permute-start.5) | collective-permute-done | bytes 131104 | tf_op jit(solution)/shard_map/ppermute | solution.py:51
  59.3 0.0 collective-permute-done.4.r_square
  59.3 0.0 collective-permute-done.6.r_lift
  59.3 0.0 collective-permute-done.7.r_along
  59.3 0.9 %shard_map.33 = f32[6,2,128,128]{3,2,1,0:T(8,128)} custom-call(f32[2,128,128]{2,1,0:T(8,128)S(1)} %get-tuple-element.11.t1, f32[3,2,128,128]{3,2,1,0:T(8,128)S(1)} %get-tuple-element.14.mine, f32[3,2,128,128]{3,2,1,0:T(8,128)S(1)} %collective-permute-done.4.r_square, f32[2,128,128]{2,1,0:T(8,128)S(1)} %collective-permute-done.5.r_cross, ...), custom_call_target="tpu_custom_call" | custom-call | bytes 1024 | tf_op jit(solution)/shard_map/pallas_call | solution.py:237
Async XLA Ops:
  3.2 28.5 %collective-permute-start = (bf16[8208,128]{1,0:T(8,128)(2,1)}, bf16[8208,128]{1,0:T(8,128)(2,1)S(1)}, u32[]{:S(2)}, u32[]{:S(2)}) collective-permute-start(bf16[8208,128]{1,0:T(8,128)(2,1)} %shard_map.28.own), channel_id=1, source_target_pairs={{0,8},{1,9},{2,10},{3,11},{4,12},{5,13},{6,14},{7,15},{8,72},{9,73... | collective-permute-start | bytes 6303752 | tf_op jit(solution)/shard_map/ppermute | solution.py:51
  5.1 32.0 %collective-permute-start.2 = (bf16[8208,128]{1,0:T(8,128)(2,1)}, bf16[8208,128]{1,0:T(8,128)(2,1)S(1)}, u32[]{:S(2)}, u32[]{:S(2)}) collective-permute-start(bf16[8208,128]{1,0:T(8,128)(2,1)} %shard_map.28.own), channel_id=1, source_target_pairs={{0,384},{1,385},{2,386},{3,387},{4,388},{5,389},{6,390},{7,391},{1... | collective-permute-start | bytes 6303752 | tf_op jit(solution)/shard_map/ppermute | solution.py:51
  7.8 29.3 %collective-permute-start.3 = (bf16[8208,128]{1,0:T(8,128)(2,1)}, bf16[8208,128]{1,0:T(8,128)(2,1)S(1)}, u32[]{:S(2)}, u32[]{:S(2)}) collective-permute-start(bf16[8208,128]{1,0:T(8,128)(2,1)} %shard_map.28.own), channel_id=1, source_target_pairs={{0,9},{1,10},{2,11},{3,12},{4,13},{5,14},{6,15},{7,8},{16,25},{17,... | collective-permute-start | bytes 6303752 | tf_op jit(solution)/shard_map/ppermute | solution.py:51
  11.0 35.5 %collective-permute-start.1 = (bf16[8208,128]{1,0:T(8,128)(2,1)}, bf16[8208,128]{1,0:T(8,128)(2,1)S(1)}, u32[]{:S(2)}, u32[]{:S(2)}) collective-permute-start(bf16[8208,128]{1,0:T(8,128)(2,1)} %shard_map.28.own), channel_id=1, source_target_pairs={{0,120},{1,121},{2,122},{3,123},{4,124},{5,125},{6,126},{7,127},{8... | collective-permute-start | bytes 6303752 | tf_op jit(solution)/shard_map/ppermute | solution.py:51
  22.6 1.6 %copy-start = (bf16[8208,128]{1,0:T(8,128)(2,1)S(1)}, bf16[8208,128]{1,0:T(8,128)(2,1)}, u32[]{:S(2)}) copy-start(bf16[8208,128]{1,0:T(8,128)(2,1)} %shard_map.28.own) | copy-start | bytes 6303748
  38.7 20.6 %collective-permute-start.6 = (f32[4,2,128,128]{3,2,1,0:T(8,128)S(1)}, f32[4,2,128,128]{3,2,1,0:T(8,128)S(1)}, u32[]{:S(2)}, u32[]{:S(2)}) collective-permute-start(f32[4,2,128,128]{3,2,1,0:T(8,128)S(1)} %get-tuple-element.16), channel_id=1, source_target_pairs={{9,0},{10,1},{11,2},{12,3},{13,4},{14,5},{15,6},{8,7},{25,16},{26,... | collective-permute-start | bytes 1572872 | tf_op jit(solution)/shard_map/ppermute | solution.py:51
  40.0 19.3 %collective-permute-start.7 = (f32[4,2,128,128]{3,2,1,0:T(8,128)S(1)}, f32[4,2,128,128]{3,2,1,0:T(8,128)S(1)}, u32[]{:S(2)}, u32[]{:S(2)}) collective-permute-start(f32[4,2,128,128]{3,2,1,0:T(8,128)S(1)} %get-tuple-element.16), channel_id=1, source_target_pairs={{384,0},{385,1},{386,2},{387,3},{388,4},{389,5},{390,6},{391,7},{4... | collective-permute-start | bytes 1572872 | tf_op jit(solution)/shard_map/ppermute | solution.py:51
  48.1 11.1 %collective-permute-start.4 = (f32[3,2,128,128]{3,2,1,0:T(8,128)S(1)}, f32[3,2,128,128]{3,2,1,0:T(8,128)S(1)}, u32[]{:S(2)}, u32[]{:S(2)}) collective-permute-start(f32[3,2,128,128]{3,2,1,0:T(8,128)S(1)} %get-tuple-element.14.mine), channel_id=1, source_target_pairs={{8,0},{9,1},{10,2},{11,3},{12,4},{13,5},{14,6},{15,7},{72,8},{73,9... | collective-permute-start | bytes 1179656 | tf_op jit(solution)/shard_map/ppermute | solution.py:51
  50.1 9.2 %collective-permute-start.5 = (f32[2,128,128]{2,1,0:T(8,128)S(1)}, f32[2,128,128]{2,1,0:T(8,128)S(1)}, u32[]{:S(2)}, u32[]{:S(2)}) collective-permute-start(f32[2,128,128]{2,1,0:T(8,128)S(1)} %get-tuple-element.15), channel_id=1, source_target_pairs={{120,0},{121,1},{122,2},{123,3},{124,4},{125,5},{126,6},{127,7},{1... | collective-permute-start | bytes 393224 | tf_op jit(solution)/shard_map/ppermute | solution.py:51

commit v4 on v3

--- a/solution.py
+++ b/solution.py
@@ -124,6 +124,20 @@
     )(own)
 
 
+def token_kernel(_, out_ref):
+    out_ref[...] = jnp.zeros_like(out_ref)
+
+
+def token(array):
+    return pl.pallas_call(
+        token_kernel,
+        in_specs=[ANY],
+        out_specs=VMEM,
+        out_shape=jax.ShapeDtypeStruct((8, LANES), F32),
+        cost_estimate=pl.CostEstimate(flops=COST, bytes_accessed=COST, transcendentals=0),
+    )(array)
+
+
 def slab(ref, index):
     return ref[pl.ds(pl.multiple_of(index * ROWS, ROWS), ROWS), :]
 
@@ -161,7 +175,7 @@
     t_ref[1] = imag.T
 
 
-def square_kernel(own, square, t_ref, b_ref, *scratch):
+def square_kernel(_, own, square, t_ref, b_ref, *scratch):
     high, core = place()
     put(t_ref, b_ref.at[0], *multiply(own, square, core == 0, jnp.where(high == core, 0, 1), *scratch))
 
@@ -248,12 +262,12 @@
 def per_device(coeffs, slab_maps):
     square, cross, along, lift = routes(*(lax.axis_size(a) for a in AXES))
     own = packed(coeffs[0, 0, 0], slab_maps[0, 0, 0])
+    from_lift = send(own, lift)
     from_square = send(own, square)
     from_cross = send(own, cross)
     from_along = send(own, along)
-    from_lift = send(own, lift)
     own = kept(own)
-    t1, results = multiplier(square_kernel, [RESULT, RESULTS], [own, from_square])
+    t1, results = multiplier(square_kernel, [RESULT, RESULTS], [token(from_lift), own, from_square])
     results, h3 = multiplier(along_kernel, [RESULTS, QUAD], [from_square, from_along, from_lift], results)
     results, h2 = multiplier(cross_kernel, [RESULTS, RESULT], [own, from_square, from_cross], results)
     back_cross = send(h2, back(cross))

time: 60.6 us -> 68.7 us (1.13)
  waiting for transfers between devices: 16.5 us -> 10.3 us
  starting transfers between devices: 33.1 us -> 39.1 us
  Pallas kernels: 8.9 us -> 13.5 us
  local copies, waits for them, and re-layouts: 1.6 us -> 5.23 us
    ppermute x8, waiting for transfers between devices: 16.5 us -> 10.3 us  [send(): return lax.ppermute(x, AXES, route)]
    ppermute x8, starting transfers between devices: 33.1 us -> 39.1 us  [send(): return lax.ppermute(x, AXES, route)]
    pallas_call x3, Pallas kernels: 4.66 us -> 8.63 us  [multiplier(): pl.pallas_call(kernel, in_specs=[VMEM] * len(operands), out_specs=[VMEM]...]
    unnamed x2 -> x10, local copies, waits for them, and re-layouts: 1.6 us -> 5.23 us
  transfers between devices with their start and end apart: 8 -> 8, of which waited for: 4 -> 4; matrix products, arithmetic and copies ran while one was open for 0% -> 0% of each run, Pallas kernels for 8% -> 14%
where the time goes in v4:
time: 68.7 us; the launch traced here: 68.3 us
  starting transfers between devices  39.1 us (57%)
  Pallas kernels  13.5 us (20%)
  waiting for transfers between devices  10.3 us (15%)
  local copies, waits for them, and re-layouts  5.23 us (8%)
    ppermute x8, starting transfers between devices, send(): return lax.ppermute(x, AXES, route)  39.1 us
    ppermute x8, waiting for transfers between devices, send(): return lax.ppermute(x, AXES, route)  10.3 us
    pallas_call x3, Pallas kernels, multiplier(): pl.pallas_call(kernel, in_specs=[VMEM] * len(operands), out_specs=[VMEM]...  8.63 us
    unnamed x10, local copies, waits for them, and re-layouts  5.23 us
    pallas_call x1, Pallas kernels, packed(): pl.pallas_call(pack_kernel, in_specs=[ANY, ANY], out_specs=ANY, out_shape...  3.17 us
  transfers between devices with their start and end apart: 8, of which 4 were waited for; matrix products, arithmetic and copies ran while one was open for 0% of the time, Pallas kernels for 14%

profile of v4, /device:TPU:6, one launch (start us, length us, event | category | flops | bytes accessed | tf_op | source)
XLA Modules:
  0.0 68.3 jit_solution(9602851853121059002)
XLA Ops:
  0.0 3.2 %shard_map.28.own = bf16[8208,128]{1,0:T(8,128)(2,1)} custom-call(bf16[128,2,4096]{2,1,0:T(2,128)(2,1)} %bitcast.3, s32[3,1,32]{2,1,0:T(1,128)} %bitcast.4), custom_call_target="tpu_custom_call" | custom-call | bytes 4194304 | tf_op jit(solution)/shard_map/pallas_call | solution.py:90
  3.2 4.3 %collective-permute-start = (bf16[8208,128]{1,0:T(8,128)(2,1)}, bf16[8208,128]{1,0:T(8,128)(2,1)}, u32[]{:S(2)}, u32[]{:S(2)}) collective-permute-start(bf16[8208,128]{1,0:T(8,128)(2,1)} %shard_map.28.own), channel_id=1, source_target_pairs={{0,9},{1,10},{2,11},{3,12},{4,13},{5,14},{6,15},{7,8},{16,25},{17,... | collective-permute-start | bytes 6303752 | tf_op jit(solution)/shard_map/ppermute | solution.py:51
  7.5 1.9 %collective-permute-start.1 = (bf16[8208,128]{1,0:T(8,128)(2,1)}, bf16[8208,128]{1,0:T(8,128)(2,1)S(1)}, u32[]{:S(2)}, u32[]{:S(2)}) collective-permute-start(bf16[8208,128]{1,0:T(8,128)(2,1)} %shard_map.28.own), channel_id=1, source_target_pairs={{0,8},{1,9},{2,10},{3,11},{4,12},{5,13},{6,14},{7,15},{8,72},{9,73... | collective-permute-start | bytes 6303752 | tf_op jit(solution)/shard_map/ppermute | solution.py:51
  9.4 2.7 %collective-permute-start.3 = (bf16[8208,128]{1,0:T(8,128)(2,1)}, bf16[8208,128]{1,0:T(8,128)(2,1)}, u32[]{:S(2)}, u32[]{:S(2)}) collective-permute-start(bf16[8208,128]{1,0:T(8,128)(2,1)} %shard_map.28.own), channel_id=1, source_target_pairs={{0,384},{1,385},{2,386},{3,387},{4,388},{5,389},{6,390},{7,391},{1... | collective-permute-start | bytes 6303752 | tf_op jit(solution)/shard_map/ppermute | solution.py:51
  12.1 12.5 %collective-permute-start.2 = (bf16[8208,128]{1,0:T(8,128)(2,1)}, bf16[8208,128]{1,0:T(8,128)(2,1)}, u32[]{:S(2)}, u32[]{:S(2)}) collective-permute-start(bf16[8208,128]{1,0:T(8,128)(2,1)} %shard_map.28.own), channel_id=1, source_target_pairs={{0,120},{1,121},{2,122},{3,123},{4,124},{5,125},{6,126},{7,127},{8... | collective-permute-start | bytes 6303752 | tf_op jit(solution)/shard_map/ppermute | solution.py:51
  24.6 0.0 copy-start.3
  24.6 1.6 %copy-done.3 = bf16[8208,128]{1,0:T(8,128)(2,1)S(1)} copy-done((bf16[8208,128]{1,0:T(8,128)(2,1)S(1)}, bf16[8208,128]{1,0:T(8,128)(2,1)}, u32[]{:S(2)}) %copy-start.3) | copy-done | bytes 2101272
  26.2 0.2 shard_map.30.own
  26.4 0.0 copy-start
  26.4 1.4 %copy-done = bf16[8208,128]{1,0:T(8,128)(2,1)} copy-done((bf16[8208,128]{1,0:T(8,128)(2,1)}, bf16[8208,128]{1,0:T(8,128)(2,1)S(1)}, u32[]{:S(2)}) %copy-start) | copy-done | bytes 2101272
  27.7 2.3 %collective-permute-done._.lift = bf16[8208,128]{1,0:T(8,128)(2,1)} collective-permute-done((bf16[8208,128]{1,0:T(8,128)(2,1)}, bf16[8208,128]{1,0:T(8,128)(2,1)}, u32[]{:S(2)}, u32[]{:S(2)}) %collective-permute-start) | collective-permute-done | bytes 2101280 | tf_op jit(solution)/shard_map/ppermute | solution.py:51
  30.0 0.6 shard_map.29._
  30.6 5.0 %collective-permute-done.1.square = bf16[8208,128]{1,0:T(8,128)(2,1)S(1)} collective-permute-done((bf16[8208,128]{1,0:T(8,128)(2,1)}, bf16[8208,128]{1,0:T(8,128)(2,1)S(1)}, u32[]{:S(2)}, u32[]{:S(2)}) %collective-permute-start.1) | collective-permute-done | bytes 2101280 | tf_op jit(solution)/shard_map/ppermute | solution.py:51
  35.6 0.0 copy-start.1
  35.6 1.6 %copy-done.1 = bf16[8208,128]{1,0:T(8,128)(2,1)S(1)} copy-done((bf16[8208,128]{1,0:T(8,128)(2,1)S(1)}, bf16[8208,128]{1,0:T(8,128)(2,1)}, u32[]{:S(2)}) %copy-start.1) | copy-done | bytes 2101272
  37.2 0.0 copy-start.4
  37.2 0.7 %copy-done.4 = f32[8,128]{1,0:T(8,128)S(1)} copy-done((f32[8,128]{1,0:T(8,128)S(1)}, f32[8,128]{1,0:T(8,128)}, u32[]{:S(2)}) %copy-start.4) | copy-done | bytes 4120
  37.9 1.5 %shard_map.31 = (f32[2,128,128]{2,1,0:T(8,128)S(1)}, f32[3,2,128,128]{3,2,1,0:T(8,128)S(1)}) custom-call(f32[8,128]{1,0:T(8,128)S(1)} %copy-done.4, bf16[8208,128]{1,0:T(8,128)(2,1)S(1)} %copy-done.1, bf16[8208,128]{1,0:T(8,128)(2,1)S(1)} %collective-permute-done.1.square), custom_call_target="tpu_custom_call" | custom-call | flops 1024 | bytes 1024 | tf_op jit(solution)/shard_map/pallas_call | solution.py:209
  39.5 0.4 collective-permute-done.3.along
  39.9 3.9 %shard_map.32 = (f32[3,2,128,128]{3,2,1,0:T(8,128)S(1)}, f32[4,2,128,128]{3,2,1,0:T(8,128)S(1)}) custom-call(bf16[8208,128]{1,0:T(8,128)(2,1)S(1)} %collective-permute-done.1.square, bf16[8208,128]{1,0:T(8,128)(2,1)} %collective-permute-done.3.along, bf16[8208,128]{1,0:T(8,128)(2,1)} %collective-permute-done._.lift, ...), custom_call_target="tpu_custom_call", output_to_operand_aliasing={{0}: (3, {})} | custom-call | flops 1024 | bytes 1024 | tf_op jit(solution)/shard_map/pallas_call | solution.py:209
  43.8 1.3 %collective-permute-start.6 = (f32[4,2,128,128]{3,2,1,0:T(8,128)S(1)}, f32[4,2,128,128]{3,2,1,0:T(8,128)S(1)}, u32[]{:S(2)}, u32[]{:S(2)}) collective-permute-start(f32[4,2,128,128]{3,2,1,0:T(8,128)S(1)} %get-tuple-element.16), channel_id=1, source_target_pairs={{9,0},{10,1},{11,2},{12,3},{13,4},{14,5},{15,6},{8,7},{25,16},{26,... | collective-permute-start | bytes 1572872 | tf_op jit(solution)/shard_map/ppermute | solution.py:51
  45.1 5.7 %collective-permute-start.7 = (f32[4,2,128,128]{3,2,1,0:T(8,128)S(1)}, f32[4,2,128,128]{3,2,1,0:T(8,128)S(1)}, u32[]{:S(2)}, u32[]{:S(2)}) collective-permute-start(f32[4,2,128,128]{3,2,1,0:T(8,128)S(1)} %get-tuple-element.16), channel_id=1, source_target_pairs={{384,0},{385,1},{386,2},{387,3},{388,4},{389,5},{390,6},{391,7},{4... | collective-permute-start | bytes 1572872 | tf_op jit(solution)/shard_map/ppermute | solution.py:51
  50.9 0.0 collective-permute-done.2.cross
  50.9 0.0 copy-done.2
  50.9 3.2 %shard_map.33 = (f32[3,2,128,128]{3,2,1,0:T(8,128)S(1)}, f32[2,128,128]{2,1,0:T(8,128)S(1)}) custom-call(bf16[8208,128]{1,0:T(8,128)(2,1)S(1)} %copy-done.2, bf16[8208,128]{1,0:T(8,128)(2,1)S(1)} %collective-permute-done.1.square, bf16[8208,128]{1,0:T(8,128)(2,1)} %collective-permute-done.2.cross, ...), custom_call_target="tpu_custom_call", output_to_operand_aliasing={{0}: (3, {})} | custom-call | flops 1024 | bytes 1024 | tf_op jit(solution)/shard_map/pallas_call | solution.py:209
  54.0 1.9 %collective-permute-start.4 = (f32[3,2,128,128]{3,2,1,0:T(8,128)S(1)}, f32[3,2,128,128]{3,2,1,0:T(8,128)S(1)}, u32[]{:S(2)}, u32[]{:S(2)}) collective-permute-start(f32[3,2,128,128]{3,2,1,0:T(8,128)S(1)} %get-tuple-element.14.mine), channel_id=1, source_target_pairs={{8,0},{9,1},{10,2},{11,3},{12,4},{13,5},{14,6},{15,7},{72,8},{73,9... | collective-permute-start | bytes 1179656 | tf_op jit(solution)/shard_map/ppermute | solution.py:51
  56.0 8.7 %collective-permute-start.5 = (f32[2,128,128]{2,1,0:T(8,128)S(1)}, f32[2,128,128]{2,1,0:T(8,128)S(1)}, u32[]{:S(2)}, u32[]{:S(2)}) collective-permute-start(f32[2,128,128]{2,1,0:T(8,128)S(1)} %get-tuple-element.15), channel_id=1, source_target_pairs={{120,0},{121,1},{122,2},{123,3},{124,4},{125,5},{126,6},{127,7},{1... | collective-permute-start | bytes 393224 | tf_op jit(solution)/shard_map/ppermute | solution.py:51
  64.7 2.6 %collective-permute-done.5.r_cross = f32[2,128,128]{2,1,0:T(8,128)S(1)} collective-permute-done((f32[2,128,128]{2,1,0:T(8,128)S(1)}, f32[2,128,128]{2,1,0:T(8,128)S(1)}, u32[]{:S(2)}, u32[]{:S(2)}) %collective-permute-start.5) | collective-permute-done | bytes 131104 | tf_op jit(solution)/shard_map/ppermute | solution.py:51
  67.3 0.0 collective-permute-done.4.r_square
  67.3 0.0 collective-permute-done.6.r_lift
  67.3 0.0 collective-permute-done.7.r_along
  67.3 0.9 %shard_map.34 = f32[6,2,128,128]{3,2,1,0:T(8,128)} custom-call(f32[2,128,128]{2,1,0:T(8,128)S(1)} %get-tuple-element.11.t1, f32[3,2,128,128]{3,2,1,0:T(8,128)S(1)} %get-tuple-element.14.mine, f32[3,2,128,128]{3,2,1,0:T(8,128)S(1)} %collective-permute-done.4.r_square, f32[2,128,128]{2,1,0:T(8,128)S(1)} %collective-permute-done.5.r_cross, ...), custom_call_target="tpu_custom_call" | custom-call | bytes 1024 | tf_op jit(solution)/shard_map/pallas_call | solution.py:251
  (1 shorter events, 0.0 us)
Async XLA Ops:
  3.2 26.8 %collective-permute-start = (bf16[8208,128]{1,0:T(8,128)(2,1)}, bf16[8208,128]{1,0:T(8,128)(2,1)}, u32[]{:S(2)}, u32[]{:S(2)}) collective-permute-start(bf16[8208,128]{1,0:T(8,128)(2,1)} %shard_map.28.own), channel_id=1, source_target_pairs={{0,9},{1,10},{2,11},{3,12},{4,13},{5,14},{6,15},{7,8},{16,25},{17,... | collective-permute-start | bytes 6303752 | tf_op jit(solution)/shard_map/ppermute | solution.py:51
  7.5 28.2 %collective-permute-start.1 = (bf16[8208,128]{1,0:T(8,128)(2,1)}, bf16[8208,128]{1,0:T(8,128)(2,1)S(1)}, u32[]{:S(2)}, u32[]{:S(2)}) collective-permute-start(bf16[8208,128]{1,0:T(8,128)(2,1)} %shard_map.28.own), channel_id=1, source_target_pairs={{0,8},{1,9},{2,10},{3,11},{4,12},{5,13},{6,14},{7,15},{8,72},{9,73... | collective-permute-start | bytes 6303752 | tf_op jit(solution)/shard_map/ppermute | solution.py:51
  9.4 30.5 %collective-permute-start.3 = (bf16[8208,128]{1,0:T(8,128)(2,1)}, bf16[8208,128]{1,0:T(8,128)(2,1)}, u32[]{:S(2)}, u32[]{:S(2)}) collective-permute-start(bf16[8208,128]{1,0:T(8,128)(2,1)} %shard_map.28.own), channel_id=1, source_target_pairs={{0,384},{1,385},{2,386},{3,387},{4,388},{5,389},{6,390},{7,391},{1... | collective-permute-start | bytes 6303752 | tf_op jit(solution)/shard_map/ppermute | solution.py:51
  12.1 38.7 %collective-permute-start.2 = (bf16[8208,128]{1,0:T(8,128)(2,1)}, bf16[8208,128]{1,0:T(8,128)(2,1)}, u32[]{:S(2)}, u32[]{:S(2)}) collective-permute-start(bf16[8208,128]{1,0:T(8,128)(2,1)} %shard_map.28.own), channel_id=1, source_target_pairs={{0,120},{1,121},{2,122},{3,123},{4,124},{5,125},{6,126},{7,127},{8... | collective-permute-start | bytes 6303752 | tf_op jit(solution)/shard_map/ppermute | solution.py:51
  24.6 1.6 %copy-start.3 = (bf16[8208,128]{1,0:T(8,128)(2,1)S(1)}, bf16[8208,128]{1,0:T(8,128)(2,1)}, u32[]{:S(2)}) copy-start(bf16[8208,128]{1,0:T(8,128)(2,1)} %shard_map.28.own) | copy-start | bytes 6303748
  26.4 1.4 %copy-start = (bf16[8208,128]{1,0:T(8,128)(2,1)}, bf16[8208,128]{1,0:T(8,128)(2,1)S(1)}, u32[]{:S(2)}) copy-start(bf16[8208,128]{1,0:T(8,128)(2,1)S(1)} %shard_map.30.own) | copy-start | bytes 6303748
  35.6 1.6 %copy-start.1 = (bf16[8208,128]{1,0:T(8,128)(2,1)S(1)}, bf16[8208,128]{1,0:T(8,128)(2,1)}, u32[]{:S(2)}) copy-start(bf16[8208,128]{1,0:T(8,128)(2,1)} %copy-done) | copy-start | bytes 6303748
  37.2 0.7 %copy-start.4 = (f32[8,128]{1,0:T(8,128)S(1)}, f32[8,128]{1,0:T(8,128)}, u32[]{:S(2)}) copy-start(f32[8,128]{1,0:T(8,128)} %shard_map.29._) | copy-start | bytes 12292
  39.9 11.0 %copy-start.2 = (bf16[8208,128]{1,0:T(8,128)(2,1)S(1)}, bf16[8208,128]{1,0:T(8,128)(2,1)}, u32[]{:S(2)}) copy-start(bf16[8208,128]{1,0:T(8,128)(2,1)} %copy-done) | copy-start | bytes 6303748
  43.8 23.5 %collective-permute-start.6 = (f32[4,2,128,128]{3,2,1,0:T(8,128)S(1)}, f32[4,2,128,128]{3,2,1,0:T(8,128)S(1)}, u32[]{:S(2)}, u32[]{:S(2)}) collective-permute-start(f32[4,2,128,128]{3,2,1,0:T(8,128)S(1)} %get-tuple-element.16), channel_id=1, source_target_pairs={{9,0},{10,1},{11,2},{12,3},{13,4},{14,5},{15,6},{8,7},{25,16},{26,... | collective-permute-start | bytes 1572872 | tf_op jit(solution)/shard_map/ppermute | solution.py:51
  45.1 22.2 %collective-permute-start.7 = (f32[4,2,128,128]{3,2,1,0:T(8,128)S(1)}, f32[4,2,128,128]{3,2,1,0:T(8,128)S(1)}, u32[]{:S(2)}, u32[]{:S(2)}) collective-permute-start(f32[4,2,128,128]{3,2,1,0:T(8,128)S(1)} %get-tuple-element.16), channel_id=1, source_target_pairs={{384,0},{385,1},{386,2},{387,3},{388,4},{389,5},{390,6},{391,7},{4... | collective-permute-start | bytes 1572872 | tf_op jit(solution)/shard_map/ppermute | solution.py:51
  54.0 13.3 %collective-permute-start.4 = (f32[3,2,128,128]{3,2,1,0:T(8,128)S(1)}, f32[3,2,128,128]{3,2,1,0:T(8,128)S(1)}, u32[]{:S(2)}, u32[]{:S(2)}) collective-permute-start(f32[3,2,128,128]{3,2,1,0:T(8,128)S(1)} %get-tuple-element.14.mine), channel_id=1, source_target_pairs={{8,0},{9,1},{10,2},{11,3},{12,4},{13,5},{14,6},{15,7},{72,8},{73,9... | collective-permute-start | bytes 1179656 | tf_op jit(solution)/shard_map/ppermute | solution.py:51
  56.0 11.3 %collective-permute-start.5 = (f32[2,128,128]{2,1,0:T(8,128)S(1)}, f32[2,128,128]{2,1,0:T(8,128)S(1)}, u32[]{:S(2)}, u32[]{:S(2)}) collective-permute-start(f32[2,128,128]{2,1,0:T(8,128)S(1)} %get-tuple-element.15), channel_id=1, source_target_pairs={{120,0},{121,1},{122,2},{123,3},{124,4},{125,5},{126,6},{127,7},{1... | collective-permute-start | bytes 393224 | tf_op jit(solution)/shard_map/ppermute | solution.py:51

commit v5 on v3

--- a/solution.py
+++ b/solution.py
@@ -8,7 +8,7 @@
 AXES = ("kx", "ky", "kz")
 BANDS, PARTS, WIDTH, SLABS, LANES = 128, 2, 4096, 32, 128
 ROWS = BANDS * PARTS
-BLOCKS = 4
+BLOCKS = 2
 PER = SLABS // BLOCKS
 TAIL = 16
 F32 = jnp.float32

time: 60.6 us -> 61 us (level)
  no operation moved by 1% of the time
where the time goes in v5:
time: 61 us; the launch traced here: 60.6 us
  starting transfers between devices  33.1 us (54%)
  waiting for transfers between devices  16.5 us (27%)
  Pallas kernels  9.3 us (15%)
  local copies, waits for them, and re-layouts  1.6 us (3%)
    ppermute x8, starting transfers between devices, send(): return lax.ppermute(x, AXES, route)  33.1 us
    ppermute x8, waiting for transfers between devices, send(): return lax.ppermute(x, AXES, route)  16.5 us
    pallas_call x3, Pallas kernels, multiplier(): pl.pallas_call(kernel, in_specs=[VMEM] * len(operands), out_specs=[VMEM]...  4.66 us
    pallas_call x1, Pallas kernels, packed(): pl.pallas_call(pack_kernel, in_specs=[ANY, ANY], out_specs=ANY, out_shape...  3.55 us
    unnamed x2, local copies, waits for them, and re-layouts  1.6 us
  transfers between devices with their start and end apart: 8, of which 4 were waited for; matrix products, arithmetic and copies ran while one was open for 0% of the time, Pallas kernels for 8%

profile of v5, /device:TPU:6, one launch (start us, length us, event | category | flops | bytes accessed | tf_op | source)
XLA Modules:
  0.0 60.6 jit_solution(12327145941641401749)
XLA Ops:
  0.0 3.5 %shard_map.28.own = bf16[8208,128]{1,0:T(8,128)(2,1)} custom-call(bf16[128,2,4096]{2,1,0:T(2,128)(2,1)} %bitcast.3, s32[3,1,32]{2,1,0:T(1,128)} %bitcast.4), custom_call_target="tpu_custom_call" | custom-call | bytes 4194304 | tf_op jit(solution)/shard_map/pallas_call | solution.py:90
  3.6 1.9 %collective-permute-start = (bf16[8208,128]{1,0:T(8,128)(2,1)}, bf16[8208,128]{1,0:T(8,128)(2,1)S(1)}, u32[]{:S(2)}, u32[]{:S(2)}) collective-permute-start(bf16[8208,128]{1,0:T(8,128)(2,1)} %shard_map.28.own), channel_id=1, source_target_pairs={{0,8},{1,9},{2,10},{3,11},{4,12},{5,13},{6,14},{7,15},{8,72},{9,73... | collective-permute-start | bytes 6303752 | tf_op jit(solution)/shard_map/ppermute | solution.py:51
  5.5 2.7 %collective-permute-start.2 = (bf16[8208,128]{1,0:T(8,128)(2,1)}, bf16[8208,128]{1,0:T(8,128)(2,1)S(1)}, u32[]{:S(2)}, u32[]{:S(2)}) collective-permute-start(bf16[8208,128]{1,0:T(8,128)(2,1)} %shard_map.28.own), channel_id=1, source_target_pairs={{0,384},{1,385},{2,386},{3,387},{4,388},{5,389},{6,390},{7,391},{1... | collective-permute-start | bytes 6303752 | tf_op jit(solution)/shard_map/ppermute | solution.py:51
  8.2 3.2 %collective-permute-start.3 = (bf16[8208,128]{1,0:T(8,128)(2,1)}, bf16[8208,128]{1,0:T(8,128)(2,1)S(1)}, u32[]{:S(2)}, u32[]{:S(2)}) collective-permute-start(bf16[8208,128]{1,0:T(8,128)(2,1)} %shard_map.28.own), channel_id=1, source_target_pairs={{0,9},{1,10},{2,11},{3,12},{4,13},{5,14},{6,15},{7,8},{16,25},{17,... | collective-permute-start | bytes 6303752 | tf_op jit(solution)/shard_map/ppermute | solution.py:51
  11.4 11.6 %collective-permute-start.1 = (bf16[8208,128]{1,0:T(8,128)(2,1)}, bf16[8208,128]{1,0:T(8,128)(2,1)S(1)}, u32[]{:S(2)}, u32[]{:S(2)}) collective-permute-start(bf16[8208,128]{1,0:T(8,128)(2,1)} %shard_map.28.own), channel_id=1, source_target_pairs={{0,120},{1,121},{2,122},{3,123},{4,124},{5,125},{6,126},{7,127},{8... | collective-permute-start | bytes 6303752 | tf_op jit(solution)/shard_map/ppermute | solution.py:51
  23.0 0.0 copy-start
  23.0 1.6 %copy-done = bf16[8208,128]{1,0:T(8,128)(2,1)S(1)} copy-done((bf16[8208,128]{1,0:T(8,128)(2,1)S(1)}, bf16[8208,128]{1,0:T(8,128)(2,1)}, u32[]{:S(2)}) %copy-start) | copy-done | bytes 2101272
  24.6 0.2 shard_map.29.own
  24.8 7.3 %collective-permute-done.square = bf16[8208,128]{1,0:T(8,128)(2,1)S(1)} collective-permute-done((bf16[8208,128]{1,0:T(8,128)(2,1)}, bf16[8208,128]{1,0:T(8,128)(2,1)S(1)}, u32[]{:S(2)}, u32[]{:S(2)}) %collective-permute-start) | collective-permute-done | bytes 2101280 | tf_op jit(solution)/shard_map/ppermute | solution.py:51
  32.1 1.6 %shard_map.30 = (f32[2,128,128]{2,1,0:T(8,128)S(1)}, f32[3,2,128,128]{3,2,1,0:T(8,128)S(1)}) custom-call(bf16[8208,128]{1,0:T(8,128)(2,1)S(1)} %shard_map.29.own, bf16[8208,128]{1,0:T(8,128)(2,1)S(1)} %collective-permute-done.square), custom_call_target="tpu_custom_call" | custom-call | flops 1024 | bytes 1024 | tf_op jit(solution)/shard_map/pallas_call | solution.py:195
  33.7 3.8 %collective-permute-done.2.along = bf16[8208,128]{1,0:T(8,128)(2,1)S(1)} collective-permute-done((bf16[8208,128]{1,0:T(8,128)(2,1)}, bf16[8208,128]{1,0:T(8,128)(2,1)S(1)}, u32[]{:S(2)}, u32[]{:S(2)}) %collective-permute-start.2) | collective-permute-done | bytes 2101280 | tf_op jit(solution)/shard_map/ppermute | solution.py:51
  37.5 0.0 collective-permute-done.3.lift
  37.5 1.6 %shard_map.31 = (f32[3,2,128,128]{3,2,1,0:T(8,128)S(1)}, f32[4,2,128,128]{3,2,1,0:T(8,128)S(1)}) custom-call(bf16[8208,128]{1,0:T(8,128)(2,1)S(1)} %collective-permute-done.square, bf16[8208,128]{1,0:T(8,128)(2,1)S(1)} %collective-permute-done.2.along, bf16[8208,128]{1,0:T(8,128)(2,1)S(1)} %collective-permute-done.3.lift, ...), custom_call_target="tpu_custom_call", output_to_operand_aliasing={{0}: (3, {})} | custom-call | flops 1024 | bytes 1024 | tf_op jit(solution)/shard_map/pallas_call | solution.py:195
  39.1 1.3 %collective-permute-start.6 = (f32[4,2,128,128]{3,2,1,0:T(8,128)S(1)}, f32[4,2,128,128]{3,2,1,0:T(8,128)S(1)}, u32[]{:S(2)}, u32[]{:S(2)}) collective-permute-start(f32[4,2,128,128]{3,2,1,0:T(8,128)S(1)} %get-tuple-element.16), channel_id=1, source_target_pairs={{9,0},{10,1},{11,2},{12,3},{13,4},{14,5},{15,6},{8,7},{25,16},{26,... | collective-permute-start | bytes 1572872 | tf_op jit(solution)/shard_map/ppermute | solution.py:51
  40.4 3.9 %collective-permute-start.7 = (f32[4,2,128,128]{3,2,1,0:T(8,128)S(1)}, f32[4,2,128,128]{3,2,1,0:T(8,128)S(1)}, u32[]{:S(2)}, u32[]{:S(2)}) collective-permute-start(f32[4,2,128,128]{3,2,1,0:T(8,128)S(1)} %get-tuple-element.16), channel_id=1, source_target_pairs={{384,0},{385,1},{386,2},{387,3},{388,4},{389,5},{390,6},{391,7},{4... | collective-permute-start | bytes 1572872 | tf_op jit(solution)/shard_map/ppermute | solution.py:51
  44.3 2.7 %collective-permute-done.1.cross = bf16[8208,128]{1,0:T(8,128)(2,1)S(1)} collective-permute-done((bf16[8208,128]{1,0:T(8,128)(2,1)}, bf16[8208,128]{1,0:T(8,128)(2,1)S(1)}, u32[]{:S(2)}, u32[]{:S(2)}) %collective-permute-start.1) | collective-permute-done | bytes 2101280 | tf_op jit(solution)/shard_map/ppermute | solution.py:51
  47.0 1.5 %shard_map.32 = (f32[3,2,128,128]{3,2,1,0:T(8,128)S(1)}, f32[2,128,128]{2,1,0:T(8,128)S(1)}) custom-call(bf16[8208,128]{1,0:T(8,128)(2,1)S(1)} %shard_map.29.own, bf16[8208,128]{1,0:T(8,128)(2,1)S(1)} %collective-permute-done.square, bf16[8208,128]{1,0:T(8,128)(2,1)S(1)} %collective-permute-done.1.cross, ...), custom_call_target="tpu_custom_call", output_to_operand_aliasing={{0}: (3, {})} | custom-call | flops 1024 | bytes 1024 | tf_op jit(solution)/shard_map/pallas_call | solution.py:195
  48.5 1.9 %collective-permute-start.4 = (f32[3,2,128,128]{3,2,1,0:T(8,128)S(1)}, f32[3,2,128,128]{3,2,1,0:T(8,128)S(1)}, u32[]{:S(2)}, u32[]{:S(2)}) collective-permute-start(f32[3,2,128,128]{3,2,1,0:T(8,128)S(1)} %get-tuple-element.14.mine), channel_id=1, source_target_pairs={{8,0},{9,1},{10,2},{11,3},{12,4},{13,5},{14,6},{15,7},{72,8},{73,9... | collective-permute-start | bytes 1179656 | tf_op jit(solution)/shard_map/ppermute | solution.py:51
  50.5 6.6 %collective-permute-start.5 = (f32[2,128,128]{2,1,0:T(8,128)S(1)}, f32[2,128,128]{2,1,0:T(8,128)S(1)}, u32[]{:S(2)}, u32[]{:S(2)}) collective-permute-start(f32[2,128,128]{2,1,0:T(8,128)S(1)} %get-tuple-element.15), channel_id=1, source_target_pairs={{120,0},{121,1},{122,2},{123,3},{124,4},{125,5},{126,6},{127,7},{1... | collective-permute-start | bytes 393224 | tf_op jit(solution)/shard_map/ppermute | solution.py:51
  57.0 2.6 %collective-permute-done.5.r_cross = f32[2,128,128]{2,1,0:T(8,128)S(1)} collective-permute-done((f32[2,128,128]{2,1,0:T(8,128)S(1)}, f32[2,128,128]{2,1,0:T(8,128)S(1)}, u32[]{:S(2)}, u32[]{:S(2)}) %collective-permute-start.5) | collective-permute-done | bytes 131104 | tf_op jit(solution)/shard_map/ppermute | solution.py:51
  59.7 0.0 collective-permute-done.4.r_square
  59.7 0.0 collective-permute-done.6.r_lift
  59.7 0.0 collective-permute-done.7.r_along
  59.7 0.9 %shard_map.33 = f32[6,2,128,128]{3,2,1,0:T(8,128)} custom-call(f32[2,128,128]{2,1,0:T(8,128)S(1)} %get-tuple-element.11.t1, f32[3,2,128,128]{3,2,1,0:T(8,128)S(1)} %get-tuple-element.14.mine, f32[3,2,128,128]{3,2,1,0:T(8,128)S(1)} %collective-permute-done.4.r_square, f32[2,128,128]{2,1,0:T(8,128)S(1)} %collective-permute-done.5.r_cross, ...), custom_call_target="tpu_custom_call" | custom-call | bytes 1024 | tf_op jit(solution)/shard_map/pallas_call | solution.py:237
Async XLA Ops:
  3.6 28.5 %collective-permute-start = (bf16[8208,128]{1,0:T(8,128)(2,1)}, bf16[8208,128]{1,0:T(8,128)(2,1)S(1)}, u32[]{:S(2)}, u32[]{:S(2)}) collective-permute-start(bf16[8208,128]{1,0:T(8,128)(2,1)} %shard_map.28.own), channel_id=1, source_target_pairs={{0,8},{1,9},{2,10},{3,11},{4,12},{5,13},{6,14},{7,15},{8,72},{9,73... | collective-permute-start | bytes 6303752 | tf_op jit(solution)/shard_map/ppermute | solution.py:51
  5.5 32.0 %collective-permute-start.2 = (bf16[8208,128]{1,0:T(8,128)(2,1)}, bf16[8208,128]{1,0:T(8,128)(2,1)S(1)}, u32[]{:S(2)}, u32[]{:S(2)}) collective-permute-start(bf16[8208,128]{1,0:T(8,128)(2,1)} %shard_map.28.own), channel_id=1, source_target_pairs={{0,384},{1,385},{2,386},{3,387},{4,388},{5,389},{6,390},{7,391},{1... | collective-permute-start | bytes 6303752 | tf_op jit(solution)/shard_map/ppermute | solution.py:51
  8.2 29.3 %collective-permute-start.3 = (bf16[8208,128]{1,0:T(8,128)(2,1)}, bf16[8208,128]{1,0:T(8,128)(2,1)S(1)}, u32[]{:S(2)}, u32[]{:S(2)}) collective-permute-start(bf16[8208,128]{1,0:T(8,128)(2,1)} %shard_map.28.own), channel_id=1, source_target_pairs={{0,9},{1,10},{2,11},{3,12},{4,13},{5,14},{6,15},{7,8},{16,25},{17,... | collective-permute-start | bytes 6303752 | tf_op jit(solution)/shard_map/ppermute | solution.py:51
  11.4 35.5 %collective-permute-start.1 = (bf16[8208,128]{1,0:T(8,128)(2,1)}, bf16[8208,128]{1,0:T(8,128)(2,1)S(1)}, u32[]{:S(2)}, u32[]{:S(2)}) collective-permute-start(bf16[8208,128]{1,0:T(8,128)(2,1)} %shard_map.28.own), channel_id=1, source_target_pairs={{0,120},{1,121},{2,122},{3,123},{4,124},{5,125},{6,126},{7,127},{8... | collective-permute-start | bytes 6303752 | tf_op jit(solution)/shard_map/ppermute | solution.py:51
  23.0 1.6 %copy-start = (bf16[8208,128]{1,0:T(8,128)(2,1)S(1)}, bf16[8208,128]{1,0:T(8,128)(2,1)}, u32[]{:S(2)}) copy-start(bf16[8208,128]{1,0:T(8,128)(2,1)} %shard_map.28.own) | copy-start | bytes 6303748
  39.1 20.6 %collective-permute-start.6 = (f32[4,2,128,128]{3,2,1,0:T(8,128)S(1)}, f32[4,2,128,128]{3,2,1,0:T(8,128)S(1)}, u32[]{:S(2)}, u32[]{:S(2)}) collective-permute-start(f32[4,2,128,128]{3,2,1,0:T(8,128)S(1)} %get-tuple-element.16), channel_id=1, source_target_pairs={{9,0},{10,1},{11,2},{12,3},{13,4},{14,5},{15,6},{8,7},{25,16},{26,... | collective-permute-start | bytes 1572872 | tf_op jit(solution)/shard_map/ppermute | solution.py:51
  40.4 19.3 %collective-permute-start.7 = (f32[4,2,128,128]{3,2,1,0:T(8,128)S(1)}, f32[4,2,128,128]{3,2,1,0:T(8,128)S(1)}, u32[]{:S(2)}, u32[]{:S(2)}) collective-permute-start(f32[4,2,128,128]{3,2,1,0:T(8,128)S(1)} %get-tuple-element.16), channel_id=1, source_target_pairs={{384,0},{385,1},{386,2},{387,3},{388,4},{389,5},{390,6},{391,7},{4... | collective-permute-start | bytes 1572872 | tf_op jit(solution)/shard_map/ppermute | solution.py:51
  48.5 11.1 %collective-permute-start.4 = (f32[3,2,128,128]{3,2,1,0:T(8,128)S(1)}, f32[3,2,128,128]{3,2,1,0:T(8,128)S(1)}, u32[]{:S(2)}, u32[]{:S(2)}) collective-permute-start(f32[3,2,128,128]{3,2,1,0:T(8,128)S(1)} %get-tuple-element.14.mine), channel_id=1, source_target_pairs={{8,0},{9,1},{10,2},{11,3},{12,4},{13,5},{14,6},{15,7},{72,8},{73,9... | collective-permute-start | bytes 1179656 | tf_op jit(solution)/shard_map/ppermute | solution.py:51
  50.5 9.2 %collective-permute-start.5 = (f32[2,128,128]{2,1,0:T(8,128)S(1)}, f32[2,128,128]{2,1,0:T(8,128)S(1)}, u32[]{:S(2)}, u32[]{:S(2)}) collective-permute-start(f32[2,128,128]{2,1,0:T(8,128)S(1)} %get-tuple-element.15), channel_id=1, source_target_pairs={{120,0},{121,1},{122,2},{123,3},{124,4},{125,5},{126,6},{127,7},{1... | collective-permute-start | bytes 393224 | tf_op jit(solution)/shard_map/ppermute | solution.py:51
